TPU v7x, 128 devices: a whole 4x4x4 slice. The times are simulated.
128 devices in a mesh: member: 4 (over z_lo, core), grid: 32 (over x, y, z_hi).
Axes of the slice: x: 4, y: 4, z: 4 (z_hi: 2, z_lo: 2; z = z_hi * 2 + z_lo), core: 2. Of those that a mesh axis runs over, the one named last changes fastest.
Arguments:
- fields: bfloat16 [32, 64, 65536], P('member', None, 'grid'), may hold values from -8 to 8
- cotangent: bfloat16 [32, 64, 65536], P('member', None, 'grid'), may hold values from -6 to 6
- w_query: bfloat16 [64, 64], replicated, may hold values from -0.75 to 0.75
- w_key: bfloat16 [64, 64], replicated, may hold values from -0.75 to 0.75
- w_value: bfloat16 [64, 64], replicated, may hold values from -0.75 to 0.75
- w_out: bfloat16 [64, 64], replicated, may hold values from -0.75 to 0.75
- w_up: bfloat16 [256, 64], replicated, may hold values from -0.75 to 0.75
- w_down: bfloat16 [64, 256], replicated, may hold values from -0.375 to 0.375
- gain_attn: float32 [64], replicated, may hold values from 0.1 to 1.9
- gain_mlp: float32 [64], replicated, may hold values from 0.1 to 1.9
Outputs:
- result: bfloat16 [32, 64, 65536], P('member', None, 'grid')
- grad_fields: bfloat16 [32, 64, 65536], P('member', None, 'grid')
- grad_w_query: float32 [64, 64], replicated
- grad_w_key: float32 [64, 64], replicated
- grad_w_value: float32 [64, 64], replicated
- grad_w_out: float32 [64, 64], replicated
- grad_w_up: float32 [256, 64], replicated
- grad_w_down: float32 [64, 256], replicated
- grad_gain_attn: float32 [64], replicated
- grad_gain_mlp: float32 [64], replicated
All inputs are finite; a program needn't handle non-finite values.
Results may differ from a plain program's by a relative error of at most 0.0076.
Values may be sent and summed in bfloat16 or wider, within the bound.
No kernel may reach another device: no remote copies, remote signals or barrier semaphores. Data moves between devices by JAX's collectives and lax.ppermute only.
A program may use at most 192 MiB of HBM per device.

v0:
```python
import jax
import jax.numpy as jnp
from jax import lax
from jax.sharding import PartitionSpec as P

HEADS = 4


norm_eps = 1e-05
lat_span = 1.4
sharpness_divisor = 32.0


def channel_norm(field, gain):
    values = field.astype(jnp.float32)
    center = values - jnp.mean(values, axis=1, keepdims=True)
    spread = lax.rsqrt(jnp.mean(center * center, axis=1, keepdims=True) + norm_eps)
    normed = center * spread
    return ((normed * gain[None, :, None]).astype(jnp.bfloat16), normed, spread)


def norm_back(grad_normed, normed, spread, gain):
    scaled = grad_normed * gain[None, :, None]
    return spread * (
        scaled
        - jnp.mean(scaled, axis=1, keepdims=True)
        - normed * jnp.mean(scaled * normed, axis=1, keepdims=True)
    )


def project(weight_matrix, field):
    return jnp.einsum("oc,mcg->mog", weight_matrix, field, preferred_element_type=jnp.float32)


def project_back(weight_matrix, grad):
    return jnp.einsum("oc,mog->mcg", weight_matrix, grad, preferred_element_type=jnp.float32)


def outer_sum(grad, field):
    return jnp.einsum("mog,mcg->oc", grad, field, preferred_element_type=jnp.float32)


def pack_sums(arrays):
    return jnp.concatenate([member_array.reshape(-1) for member_array in arrays])


def unpack_sums(flattened, templates):
    pieces = []
    offset = 0
    for template in templates:
        length = template.size
        pieces.append(flattened[offset : offset + length].reshape(template.shape))
        offset = offset + length
    return tuple(pieces)


def split_heads(tensor):
    return tensor.reshape(tensor.shape[0], HEADS, tensor.shape[1] // HEADS, tensor.shape[2])


def score_terms(left, right):
    return jnp.einsum(
        "ihdg,jhdg->hij", split_heads(left), split_heads(right), preferred_element_type=jnp.float32
    )


def combine(weights, right):
    merged = jnp.einsum(
        "hij,jhdg->ihdg", weights, split_heads(right), preferred_element_type=jnp.float32
    )
    return merged.reshape(merged.shape[0], right.shape[1], right.shape[2])


def spread_back(weights, left):
    merged = jnp.einsum(
        "hij,ihdg->jhdg", weights, split_heads(left), preferred_element_type=jnp.float32
    )
    return merged.reshape(merged.shape[0], left.shape[1], left.shape[2])


def latitude(start, width, tile):
    position = start.astype(jnp.float32) + jnp.arange(width, dtype=jnp.float32)
    return jnp.cos(lat_span * (position + 0.5) / tile)


def softmax_probs(scores):
    expo = jnp.exp(scores)
    probs = expo / jnp.sum(expo, axis=2, keepdims=True)
    return (probs, probs.astype(jnp.bfloat16))


def score_grad(probs, dots, attention_divisor):
    return (
        attention_divisor * probs * (dots - jnp.sum(probs * dots, axis=2, keepdims=True))
    ).astype(jnp.bfloat16)


def project_fields(rows, lat, w_query, w_key, w_value, gain_attn):
    normed1, hat1, spread1 = channel_norm(rows, gain_attn)
    query = (project(w_query, normed1) * lat).astype(jnp.bfloat16)
    key = project(w_key, normed1).astype(jnp.bfloat16)
    value = project(w_value, normed1).astype(jnp.bfloat16)
    return (normed1, hat1, spread1, query, key, value)


def later_half(rows, mixed, grads_in, w_out, w_up, w_down, gain_mlp):
    resid = rows.astype(jnp.float32) + project(w_out, mixed)
    normed2, hat2, spread2 = channel_norm(resid, gain_mlp)
    inner = project(w_up, normed2)
    sig = jax.nn.sigmoid(inner)
    hidden = (inner * sig).astype(jnp.bfloat16)
    result = (resid + project(w_down, hidden)).astype(jnp.bfloat16)
    grad_inner = (project_back(w_down, grads_in) * sig * (1.0 + inner * (1.0 - sig))).astype(
        jnp.bfloat16
    )
    grad_normed2 = project_back(w_up, grad_inner)
    grad_resid = grads_in.astype(jnp.float32) + norm_back(grad_normed2, hat2, spread2, gain_mlp)
    grad_resid_b = grad_resid.astype(jnp.bfloat16)
    grad_mixed = project_back(w_out, grad_resid_b).astype(jnp.bfloat16)
    grads = (
        outer_sum(grad_resid_b, mixed),
        outer_sum(grad_inner, normed2),
        outer_sum(grads_in, hidden),
        jnp.sum(grad_normed2 * hat2, axis=(0, 2)),
    )
    return (result, grad_resid, grad_mixed, grads)


def first_back(
    normed1,
    hat1,
    spread1,
    grad_query,
    grad_key,
    grad_value,
    grad_resid,
    w_query,
    w_key,
    w_value,
    gain_attn,
):
    grad_normed1 = (
        project_back(w_query, grad_query)
        + project_back(w_key, grad_key)
        + project_back(w_value, grad_value)
    )
    grad_rows = (grad_resid + norm_back(grad_normed1, hat1, spread1, gain_attn)).astype(
        jnp.bfloat16
    )
    grads = (
        outer_sum(grad_query, normed1),
        outer_sum(grad_key, normed1),
        outer_sum(grad_value, normed1),
        jnp.sum(grad_normed1 * hat1, axis=(0, 2)),
    )
    return (grad_rows, grads)


def shards(fields, cotangent, w_query, w_key, w_value, w_out, w_up, w_down, gain_attn, gain_mlp):
    tile = fields.shape[2]
    groups = lax.axis_size("member")
    location_number = tile * lax.axis_size("grid")
    features_per_part = fields.shape[1] // HEADS
    attention_divisor = sharpness_divisor / (features_per_part * location_number)
    rows = lax.all_to_all(fields, "member", split_axis=2, concat_axis=0, tiled=True)
    width = tile // groups
    lat = latitude(lax.axis_index("member") * width, width, tile)
    normed1, hat1, spread1, query, key, value = project_fields(
        rows, lat, w_query, w_key, w_value, gain_attn
    )
    scores = lax.psum(score_terms(query, key), ("member", "grid")) * attention_divisor
    probs, probs_b = softmax_probs(scores)
    mixed = combine(probs_b, value).astype(jnp.bfloat16)
    grads_in = lax.all_to_all(cotangent, "member", split_axis=2, concat_axis=0, tiled=True)
    result, grad_resid, grad_mixed, mlp_grads = later_half(
        rows, mixed, grads_in, w_out, w_up, w_down, gain_mlp
    )
    result_out = lax.all_to_all(result, "member", split_axis=0, concat_axis=2, tiled=True)
    terms = score_terms(grad_mixed, value)
    dots = lax.psum(terms, ("member", "grid"))
    grad_scores = score_grad(probs, dots, attention_divisor)
    grad_value = spread_back(probs_b, grad_mixed).astype(jnp.bfloat16)
    grad_query = (combine(grad_scores, key) * lat).astype(jnp.bfloat16)
    grad_key = spread_back(grad_scores, query).astype(jnp.bfloat16)
    grad_rows, attn_grads = first_back(
        normed1,
        hat1,
        spread1,
        grad_query,
        grad_key,
        grad_value,
        grad_resid,
        w_query,
        w_key,
        w_value,
        gain_attn,
    )
    upstream_adjoint = lax.all_to_all(grad_rows, "member", split_axis=0, concat_axis=2, tiled=True)
    joined = tuple(attn_grads) + tuple(mlp_grads)
    summed = lax.psum(pack_sums(joined), ("member", "grid"))
    unpacked = unpack_sums(summed, joined)
    attn_grads = unpacked[:4]
    mlp_grads = unpacked[4:]
    query_weight_gradient, grad_wk, grad_wv, grad_ga = attn_grads
    grad_wo, grad_wu, grad_wd, grad_gm = mlp_grads
    return (
        result_out,
        upstream_adjoint,
        query_weight_gradient,
        grad_wk,
        grad_wv,
        grad_wo,
        grad_wu,
        grad_wd,
        grad_ga,
        grad_gm,
    )


def solution(mesh):
    return jax.shard_map(
        shards,
        mesh=mesh,
        in_specs=(
            P("member", None, "grid"),
            P("member", None, "grid"),
            P(),
            P(),
            P(),
            P(),
            P(),
            P(),
            P(),
            P(),
        ),
        out_specs=(
            P("member", None, "grid"),
            P("member", None, "grid"),
            P(),
            P(),
            P(),
            P(),
            P(),
            P(),
            P(),
            P(),
        ),
        check_vma=False,
    )
```

profile of v0, /device:TPU:1, one launch (start us, length us, event | category | flops | bytes accessed | tf_op | source)
XLA Modules:
  0.0 491.6 jit_solution(10707394243371950446)
XLA Ops:
  7.2 5.6 %copy.80 = bf16[8,64,2048]{1,0,2:T(8,128)(2,1)} copy(bf16[8,64,2048]{2,1,0:T(8,128)(2,1)} %param.10) | data formatting | bytes 4194304 | tf_op args[0]
  12.8 5.9 %reshape.237 = bf16[4,2,131072]{2,1,0:T(2,128)(2,1)} reshape(bf16[2048,8,64]{2,1,0:T(8,128)(2,1)} %bitcast.228) | data formatting | bytes 4194304
  18.7 5.0 %all-to-all-start = ((bf16[4,2,131072]{2,1,0:T(2,128)(2,1)}), bf16[4,2,131072]{2,1,0:T(2,128)(2,1)S(1)}, u32[]{:S(2)}, u32[]{:S(2)}) async-start(bf16[4,2,131072]{2,1,0:T(2,128)(2,1)} %reshape.237), calls=%async_computation | async-start | bytes 4194304 | tf_op jit(solution)/shard_map/all_to_all | solution.py:165
  23.7 5.6 %copy.88 = bf16[8,64,2048]{1,0,2:T(8,128)(2,1)} copy(bf16[8,64,2048]{2,1,0:T(8,128)(2,1)} %param.11) | data formatting | bytes 4194304 | tf_op args[1]
  29.4 5.9 %reshape.239 = bf16[4,2,131072]{2,1,0:T(2,128)(2,1)} reshape(bf16[2048,8,64]{2,1,0:T(8,128)(2,1)} %bitcast.229) | data formatting | bytes 4194304
  35.3 13.2 %all-to-all-done = bf16[4,2,131072]{2,1,0:T(2,128)(2,1)S(1)} async-done(((bf16[4,2,131072]{2,1,0:T(2,128)(2,1)}), bf16[4,2,131072]{2,1,0:T(2,128)(2,1)S(1)}, u32[]{:S(2)}, u32[]{:S(2)}) %all-to-all-start) | async-done | bytes 2097184 | tf_op jit(solution)/shard_map/all_to_all | solution.py:165
  48.6 5.5 %all-to-all-start.2 = ((bf16[4,2,131072]{2,1,0:T(2,128)(2,1)}), bf16[4,2,131072]{2,1,0:T(2,128)(2,1)}, u32[]{:S(2)}, u32[]{:S(2)}) async-start(bf16[4,2,131072]{2,1,0:T(2,128)(2,1)} %reshape.239), calls=%async_computation.2 | async-start | bytes 4194304 | tf_op jit(solution)/shard_map/all_to_all | solution.py:174
  54.1 4.0 reshape.238
  58.1 6.1 %copy.81 = f32[8,64,4,512]{3,1,0,2:T(8,128)} copy(bf16[8,64,4,512]{1,0,3,2:T(8,128)(2,1)} %bitcast.230) | data formatting | bytes 6291456 | tf_op jit(solution)/shard_map/convert_element_type | solution.py:107
  72.0 4.4 fusion.38
  76.5 68.5 %psum.21 = f32[4,32,32]{2,1,0:T(8,128)S(1)} all-reduce(f32[4,32,32]{2,1,0:T(8,128)S(1)} %fusion.38), channel_id=1, replica_groups=mesh['member'=4,'grid'=32] {'member','grid'}, use_global_device_ids=true, to_apply=%region_2.0 | all-reduce | flops 4096 | bytes 32768 | tf_op jit(solution)/shard_map/psum | solution.py:171
  147.1 5.8 %reshape.240 = bf16[2048,8,64]{2,1,0:T(8,128)(2,1)} reshape(bf16[4,2,131072]{2,1,0:T(2,128)(2,1)} %all-to-all-done.2) | data formatting | bytes 4194304
  152.9 5.5 %copy.89 = bf16[8,64,4,512]{3,1,0,2:T(8,128)(2,1)} copy(bf16[8,64,4,512]{1,0,3,2:T(8,128)(2,1)} %bitcast.227) | data formatting | bytes 4194304 | tf_op jit(solution)/shard_map/all_to_all | solution.py:174
  158.4 3.4 convolution_convert_fusion
  165.6 8.8 %fusion.6 = (bf16[32,256,512]{1,2,0:T(8,128)(2,1)S(1)}, f32[32,512,256]{2,1,0:T(8,128)}) fusion(bf16[256,64]{0,1:T(8,128)(2,1)S(1)} %copy-done, f32[32,64,512]{2,1,0:T(8,128)S(1)} %get-tuple-element.47, f32[64]{0:T(128)S(1)} %copy-done.19, f32[32,512]{1,0:T(8,128)S(1)} %add_rsqrt_fusion, f32[32,512]{1,0:T(8,128)S(1)} %broadcast_multiply_fusion.4), kind=kOutput, calls=%fused_computation.10 | convolution fusion | flops 562036736 | bytes 29524224 | tf_op jit(solution)/shard_map/oc,mcg->mog/dot_general | solution.py:32
  176.0 4.0 fusion.10
  180.0 10.2 %fusion.2 = bf16[32,256,512]{1,2,0:T(8,128)(2,1)S(1)} fusion(f32[32,512,256]{2,1,0:T(8,128)} %get-tuple-element.49, bf16[32,64,512]{2,1,0:T(8,128)(2,1)S(1)} %bitcast.224, bf16[64,256]{1,0:T(8,128)(2,1)S(1)} %copy-done.17), kind=kOutput, calls=%fused_computation.3 | convolution fusion | flops 574619648 | bytes 27295744 | tf_op jit(solution)/shard_map/oc,mog->mcg/dot_general | solution.py:36
  195.9 5.4 %fusion.9 = (f32[64]{0:T(128)S(1)}, f32[32,512]{1,0:T(8,128)S(1)}, f32[32,512]{1,0:T(8,128)S(1)}, f32[32,512,64]{1,2,0:T(8,128)S(1)}) fusion(f32[32,64,512]{2,1,0:T(8,128)S(1)} %get-tuple-element.47, f32[32,512]{1,0:T(8,128)S(1)} %add_rsqrt_fusion, f32[32,512]{1,0:T(8,128)S(1)} %broadcast_multiply_fusion.4, f32[64]{0:T(128)S(1)} %copy-done.19, ...), kind=kOutput, calls=%fused_computation.17 | convolution fusion | flops 545226688 | bytes 17072640 | tf_op jit(solution)/shard_map/oc,mog->mcg/dot_general | solution.py:36
  207.7 4.4 fusion.43
  214.9 62.6 %psum.22 = f32[4,32,32]{2,1,0:T(8,128)S(1)} all-reduce(f32[4,32,32]{2,1,0:T(8,128)S(1)} %fusion.43), channel_id=1, replica_groups=mesh['member'=4,'grid'=32] {'member','grid'}, use_global_device_ids=true, to_apply=%region_8.0 | all-reduce | flops 4096 | bytes 32768 | tf_op jit(solution)/shard_map/psum | solution.py:180
  277.5 4.4 convolution_convert_fusion.4
  282.0 5.3 %fusion.32 = f32[4,16,512,32]{2,3,1,0:T(8,128)} fusion(bf16[32,4,16,512]{3,2,1,0:T(8,128)(2,1)} %bitcast.236, f32[4,32,32]{2,1,0:T(8,128)S(1)} %psum.22, f32[4,32,32]{2,1,0:T(8,128)S(1)} %psum.21, f32[4,32]{1,0:T(4,128)S(1)} %fusion.69), kind=kOutput, calls=%fused_computation.62 | convolution fusion | flops 67145888 | bytes 6324736 | tf_op jit(solution)/shard_map/hij,jhdg->ihdg/dot_general | solution.py:68
  287.4 5.3 %all-to-all-start.1 = ((bf16[32,64,512]{2,1,0:T(8,128)(2,1)}), bf16[32,64,512]{2,1,0:T(8,128)(2,1)}, u32[]{:S(2)}, u32[]{:S(2)}) async-start(bf16[32,64,512]{2,1,0:T(8,128)(2,1)} %fusion.10), calls=%async_computation.1 | async-start | bytes 4194304 | tf_op jit(solution)/shard_map/all_to_all | solution.py:178
  292.8 4.0 fusion.58
  296.9 5.2 %fusion.64 = f32[32,512,64]{1,2,0:T(8,128)S(1)} fusion(f32[32,64,512]{2,0,1:T(8,128)} %bitcast.221, f32[512]{0:T(512)S(1)} %multiply_cosine_fusion, bf16[64,64]{1,0:T(8,128)(2,1)S(1)} %copy-done.14), kind=kOutput, calls=%fused_computation.82 | convolution fusion | flops 136314880 | bytes 8398848 | tf_op jit(solution)/shard_map/oc,mog->mcg/dot_general | solution.py:36
  304.9 3.5 fusion.8
  308.5 3.8 add_convert_fusion
  312.3 5.2 %all-to-all-done.1 = bf16[32,64,512]{2,1,0:T(8,128)(2,1)} async-done(((bf16[32,64,512]{2,1,0:T(8,128)(2,1)}), bf16[32,64,512]{2,1,0:T(8,128)(2,1)}, u32[]{:S(2)}, u32[]{:S(2)}) %all-to-all-start.1) | async-done | bytes 2097184 | tf_op jit(solution)/shard_map/all_to_all | solution.py:178
  317.6 5.5 %all-to-all-start.3 = ((bf16[32,64,512]{2,1,0:T(8,128)(2,1)}), bf16[32,64,512]{2,1,0:T(8,128)(2,1)}, u32[]{:S(2)}, u32[]{:S(2)}) async-start(bf16[32,64,512]{2,1,0:T(8,128)(2,1)} %add_convert_fusion), calls=%async_computation.3 | async-start | bytes 4194304 | tf_op jit(solution)/shard_map/all_to_all | solution.py:198
  323.1 4.0 fusion.55
  327.1 4.6 convolution_bitcast_fusion.2
  332.7 137.9 %all-reduce.2.cloned.1.call-done = f32[49280]{0:T(1024)} async-done(((f32[49280]{0:T(1024)}), f32[49280]{0:T(1024)}) %all-reduce.2.cloned.1.call-update) | async-done | bytes 197136 | tf_op jit(solution)/shard_map/psum | solution.py:200
  (87 shorter events, 48.0 us)
Async XLA Ops:
  7.2 158.4 %copy-start = (bf16[256,64]{0,1:T(8,128)(2,1)S(1)}, bf16[256,64]{0,1:T(8,128)(2,1)}, u32[]{:S(2)}) copy-start(bf16[256,64]{0,1:T(8,128)(2,1)} %param.16) | copy-start | bytes 98308
  18.7 29.8 %all-to-all-start = ((bf16[4,2,131072]{2,1,0:T(2,128)(2,1)}), bf16[4,2,131072]{2,1,0:T(2,128)(2,1)S(1)}, u32[]{:S(2)}, u32[]{:S(2)}) async-start(bf16[4,2,131072]{2,1,0:T(2,128)(2,1)} %reshape.237), calls=%async_computation | async-start | bytes 4194304 | tf_op jit(solution)/shard_map/all_to_all | solution.py:165
  48.6 98.5 %all-to-all-start.2 = ((bf16[4,2,131072]{2,1,0:T(2,128)(2,1)}), bf16[4,2,131072]{2,1,0:T(2,128)(2,1)}, u32[]{:S(2)}, u32[]{:S(2)}) async-start(bf16[4,2,131072]{2,1,0:T(2,128)(2,1)} %reshape.239), calls=%async_computation.2 | async-start | bytes 4194304 | tf_op jit(solution)/shard_map/all_to_all | solution.py:174
  64.2 3.4 copy-start.1
  64.2 4.2 copy-start.18
  68.4 0.9 copy-start.15
  68.4 1.6 copy-start.14
  70.0 1.3 copy-start.9
  70.7 1.3 copy-start.11
  70.7 74.4 %copy-start.16 = (bf16[64,64]{1,0:T(8,128)(2,1)S(1)}, bf16[64,64]{1,0:T(8,128)(2,1)}, u32[]{:S(2)}) copy-start(bf16[64,64]{1,0:T(8,128)(2,1)} %param.14) | copy-start | bytes 24580
  152.9 8.9 %copy-start.13 = (bf16[64,64]{1,0:T(8,128)(2,1)S(1)}, bf16[64,64]{1,0:T(8,128)(2,1)}, u32[]{:S(2)}) copy-start(bf16[64,64]{1,0:T(8,128)(2,1)} %param.15) | copy-start | bytes 24580
  158.4 3.4 copy-start.2
  164.8 0.8 copy-start.19
  165.6 8.8 %copy-start.6 = (bf16[8,64,4,512]{3,1,0,2:T(8,128)(2,1)S(1)}, bf16[8,64,4,512]{3,1,0,2:T(8,128)(2,1)}, u32[]{:S(2)}) copy-start(bf16[8,64,4,512]{3,1,0,2:T(8,128)(2,1)} %copy.89) | copy-start | bytes 6291460
  174.4 1.6 copy-start.17
  190.2 3.2 copy-start.8
  203.5 3.4 copy-start.4
  206.1 1.6 copy-start.10
  287.4 30.2 %all-to-all-start.1 = ((bf16[32,64,512]{2,1,0:T(8,128)(2,1)}), bf16[32,64,512]{2,1,0:T(8,128)(2,1)}, u32[]{:S(2)}, u32[]{:S(2)}) async-start(bf16[32,64,512]{2,1,0:T(8,128)(2,1)} %fusion.10), calls=%async_computation.1 | async-start | bytes 4194304 | tf_op jit(solution)/shard_map/all_to_all | solution.py:178
  296.9 5.2 %copy-start.7 = (bf16[4,16,512,32]{2,3,1,0:T(8,128)(2,1)S(1)}, bf16[4,16,512,32]{2,3,1,0:T(8,128)(2,1)}, u32[]{:S(2)}) copy-start(bf16[4,16,512,32]{2,3,1,0:T(8,128)(2,1)} %convolution_convert_fusion.4) | copy-start | bytes 6291460
  302.1 2.2 copy-start.3
  302.1 2.9 copy-start.12
  304.9 3.6 copy-start.5
  317.6 163.5 %all-to-all-start.3 = ((bf16[32,64,512]{2,1,0:T(8,128)(2,1)}), bf16[32,64,512]{2,1,0:T(8,128)(2,1)}, u32[]{:S(2)}, u32[]{:S(2)}) async-start(bf16[32,64,512]{2,1,0:T(8,128)(2,1)} %add_convert_fusion), calls=%async_computation.3 | async-start | bytes 4194304 | tf_op jit(solution)/shard_map/all_to_all | solution.py:198
  323.1 147.4 %all-reduce.2.cloned.1.call-start = ((), (), s32[]{:S(2)}) async-start(), calls=%async_computation.4 | async-start | bytes 401408 | tf_op jit(solution)/shard_map/psum | solution.py:200
Sparse Core Ops, SparseCore 0:
  332.8 137.6 all-reduce.1
where the time goes:
time: 496 us; the launch traced here: 492 us
  waiting for transfers between devices  156 us (31%)
  blocking collectives  131 us (26%)
  matrix products  90 us (18%)
  local copies, waits for them, and re-layouts  66.4 us (13%)
  starting transfers between devices  21.3 us (4%)
  between operations  14.9 us (3%)
  other arithmetic  11.6 us (2%)
    psum x1, waiting for transfers between devices, shards(): summed = lax.psum(pack_sums(joined), ('member', 'grid'))  138 us
    psum x1, blocking collectives, shards(): lax.psum(score_terms(query, key), ('member', 'grid')) * attention_divisor  68.5 us
    psum x1, blocking collectives, shards(): dots = lax.psum(terms, ('member', 'grid'))  62.6 us
    unnamed x48, local copies, waits for them, and re-layouts  40.6 us
    dot_general x6, matrix products, project_back(): jnp.einsum('oc,mog->mcg', weight_matrix, grad, preferred_element_type=jnp...  26.8 us
    dot_general x6, matrix products, outer_sum(): jnp.einsum('mog,mcg->oc', grad, field, preferred_element_type=jnp.float32)  19.2 us
    dot_general x6, matrix products, project(): jnp.einsum('oc,mcg->mog', weight_matrix, field, preferred_element_type=jn...  19.1 us
    all_to_all x1, waiting for transfers between devices, shards(): lax.all_to_all(fields, 'member', split_axis=2, concat_axis=0, tiled=True)  13.2 us
  transfers between devices with their start and end apart: 5, of which 3 were waited for; matrix products, arithmetic and copies ran while one was open for 15% of the time, Pallas kernels for 0%

commit v1 on v0

v1 whole, which is shorter than its diff:
```python
import functools

import jax
import jax.numpy as jnp
from jax import lax
from jax.experimental import pallas as pl
from jax.experimental.pallas import tpu as pltpu
from jax.sharding import PartitionSpec as P

HEADS = 4

norm_eps = 1e-05
lat_span = 1.4
sharpness_divisor = 32.0

VMEM_LIMIT = 56 * 1024 * 1024
f32 = jnp.float32
bf16 = jnp.bfloat16


def dot(left, right):
    return lax.dot_general(left, right, (((1,), (0,)), ((), ())), preferred_element_type=f32)


def dot_t(left, right):
    return lax.dot_general(left, right, (((1,), (1,)), ((), ())), preferred_element_type=f32)


def channel_hat(values):
    center = values - jnp.mean(values, axis=0, keepdims=True)
    spread = lax.rsqrt(jnp.mean(center * center, axis=0, keepdims=True) + norm_eps)
    return center * spread, spread


def norm_back(scaled, hat, spread):
    return spread * (
        scaled
        - jnp.mean(scaled, axis=0, keepdims=True)
        - hat * jnp.mean(scaled * hat, axis=0, keepdims=True)
    )


def member_rows(members, part):
    shape = (members * part, members)
    row = lax.broadcasted_iota(jnp.int32, shape, 0)
    column = lax.broadcasted_iota(jnp.int32, shape, 1)
    return row // part == column


def same_channel(members, part):
    shape = (members * part, members * part)
    row = lax.broadcasted_iota(jnp.int32, shape, 0)
    column = lax.broadcasted_iota(jnp.int32, shape, 1)
    return row % part == column % part


def head_rows(ref, head, part):
    members, _, cells = ref.shape
    return ref[:, head * part : (head + 1) * part, :].reshape(members * part, cells)


def pair_sums(left_ref, right_ref, out_ref):
    members, channels, _ = left_ref.shape
    part = channels // HEADS
    same = same_channel(members, part)
    collect = member_rows(members, part).astype(f32)
    sums = []
    for head in range(HEADS):
        pairs = dot_t(head_rows(left_ref, head, part), head_rows(right_ref, head, part))
        pairs = jnp.where(same, pairs, 0.0).reshape(members, part, members * part)
        lanes = jnp.sum(pairs, axis=1)
        sums.append(
            lax.dot_general(
                lanes,
                collect,
                (((1,), (0,)), ((), ())),
                precision=lax.Precision.HIGHEST,
                preferred_element_type=f32,
            )
        )
    out_ref[...] = jnp.concatenate(sums, axis=1)


def softmax_probs(score_sums, head, divisor):
    members = score_sums.shape[0]
    expo = jnp.exp(score_sums[:, head * members : (head + 1) * members] * divisor)
    return expo / jnp.sum(expo, axis=1, keepdims=True)


def per_channel(weights, spread, same, transposed):
    rows = (dot_t if transposed else dot)(spread, weights).astype(bf16)
    return jnp.where(same, dot_t(rows, spread), 0.0).astype(bf16)


def first_kernel(
    place, x0, x1, x2, x3, w_qkv, gain, lat, rows_out, q_out, k_out, v_out, sums_out, q_all, k_all
):
    step = pl.program_id(0)
    block, channels, _ = x0.shape
    base = (place[0] ^ step) * block

    def work(x_ref):
        def member(i, carry):
            raw = x_ref[i]
            hat, _ = channel_hat(raw.astype(f32))
            normed = (hat * gain[...]).astype(bf16)
            qkv = dot(w_qkv[...], normed)
            query = (qkv[:channels] * lat[...]).astype(bf16)
            key = qkv[channels : 2 * channels].astype(bf16)
            rows_out[i] = raw
            q_out[i] = query
            k_out[i] = key
            v_out[i] = qkv[2 * channels :].astype(bf16)
            q_all[base + i] = query
            k_all[base + i] = key
            return carry

        lax.fori_loop(0, block, member, 0, unroll=2)

    for d, x_ref in enumerate((x0, x1, x2, x3)):
        pl.when(step == d)(functools.partial(work, x_ref))

    @pl.when(step == pl.num_programs(0) - 1)
    def _():
        pair_sums(q_all, k_all, sums_out)


def middle_kernel(
    divisor,
    sums,
    v_all,
    rows,
    cot,
    w_out,
    w_out_t,
    w_up,
    w_up_t,
    w_down,
    w_down_t,
    gain,
    result_out,
    resid_out,
    mixed_grad_out,
    dots_out,
    g_up_out,
    g_down_out,
    g_out_out,
    g_gain_out,
    mixed_all,
    grad_all,
):
    step = pl.program_id(0)
    block, channels, cells = rows.shape
    members = v_all.shape[0]
    part = channels // HEADS

    @pl.when(step == 0)
    def _():
        spread = member_rows(members, part).astype(bf16)
        same = same_channel(members, part)
        score_sums = sums[...]
        for head in range(HEADS):
            probs = softmax_probs(score_sums, head, divisor).astype(bf16)
            matrix = per_channel(probs, spread, same, False)
            mixed = dot(matrix, head_rows(v_all, head, part)).astype(bf16)
            mixed_all[:, head * part : (head + 1) * part, :] = mixed.reshape(members, part, cells)
        g_up_out[...] = jnp.zeros_like(g_up_out)
        g_down_out[...] = jnp.zeros_like(g_down_out)
        g_out_out[...] = jnp.zeros_like(g_out_out)
        g_gain_out[...] = jnp.zeros_like(g_gain_out)

    base = step * block

    def member(i, carry):
        mixed = mixed_all[base + i]
        grads_in = cot[i]
        resid = rows[i].astype(f32) + dot(w_out[...], mixed)
        hat, spread = channel_hat(resid)
        normed = (hat * gain[...]).astype(bf16)
        inner = dot(w_up[...], normed)
        sig = 0.5 * jnp.tanh(0.5 * inner) + 0.5
        hidden = (inner * sig).astype(bf16)
        result_out[i] = (resid + dot(w_down[...], hidden)).astype(bf16)
        grad_inner = (
            dot(w_down_t[...], grads_in) * (sig * (1.0 + inner * (1.0 - sig)))
        ).astype(bf16)
        grad_normed = dot(w_up_t[...], grad_inner)
        grad_resid = grads_in.astype(f32) + norm_back(grad_normed * gain[...], hat, spread)
        resid_out[i] = grad_resid
        grad_resid_b = grad_resid.astype(bf16)
        grad_mixed = dot(w_out_t[...], grad_resid_b).astype(bf16)
        mixed_grad_out[i] = grad_mixed
        grad_all[base + i] = grad_mixed
        g_up_out[...] += dot_t(grad_inner, normed)
        g_down_out[...] += dot_t(hidden, grads_in)
        g_out_out[...] += dot_t(grad_resid_b, mixed)
        g_gain_out[...] += jnp.sum(grad_normed * hat, axis=1, keepdims=True)
        return carry

    lax.fori_loop(0, block, member, 0, unroll=2)

    @pl.when(step == pl.num_programs(0) - 1)
    def _():
        pair_sums(grad_all, v_all, dots_out)


def last_kernel(
    divisor,
    sums,
    dots,
    q_all,
    k_all,
    grad_all,
    rows,
    resid,
    w_qkv_t,
    gain,
    lat,
    rows_out,
    g_qkv_out,
    g_gain_out,
    qkv_all,
):
    step = pl.program_id(0)
    block, channels, cells = rows.shape
    members = q_all.shape[0]
    part = channels // HEADS

    @pl.when(step == 0)
    def _():
        spread = member_rows(members, part).astype(bf16)
        same = same_channel(members, part)
        score_sums = sums[...]
        dot_sums = dots[...]
        for head in range(HEADS):
            probs = softmax_probs(score_sums, head, divisor)
            own = dot_sums[:, head * members : (head + 1) * members]
            grad_scores = (
                divisor * probs * (own - jnp.sum(probs * own, axis=1, keepdims=True))
            ).astype(bf16)
            probs = probs.astype(bf16)

            def place(offset, value, head=head):
                start = offset + head * part
                qkv_all[:, start : start + part, :] = value.astype(bf16).reshape(
                    members, part, cells
                )

            matrix = per_channel(grad_scores, spread, same, False)
            place(0, dot(matrix, head_rows(k_all, head, part)) * lat[...])
            matrix = per_channel(grad_scores, spread, same, True)
            place(channels, dot(matrix, head_rows(q_all, head, part)))
            matrix = per_channel(probs, spread, same, True)
            place(2 * channels, dot(matrix, head_rows(grad_all, head, part)))
        g_qkv_out[...] = jnp.zeros_like(g_qkv_out)
        g_gain_out[...] = jnp.zeros_like(g_gain_out)

    base = step * block

    def member(i, carry):
        hat, spread = channel_hat(rows[i].astype(f32))
        normed = (hat * gain[...]).astype(bf16)
        qkv = qkv_all[base + i]
        grad_normed = dot(w_qkv_t[...], qkv)
        rows_out[i] = (resid[i] + norm_back(grad_normed * gain[...], hat, spread)).astype(bf16)
        g_qkv_out[...] += dot_t(qkv, normed)
        g_gain_out[...] += jnp.sum(grad_normed * hat, axis=1, keepdims=True)
        return carry

    lax.fori_loop(0, block, member, 0, unroll=2)


def params():
    return pltpu.CompilerParams(
        vmem_limit_bytes=VMEM_LIMIT, dimension_semantics=("arbitrary",)
    )


def whole(array):
    return pl.BlockSpec(array.shape, lambda step, *_: (0,) * array.ndim)


def shape(dims, dtype):
    return jax.ShapeDtypeStruct(dims, dtype)


def first_call(place, blocks, w_qkv, gain, lat):
    block, channels, cells = blocks[0].shape
    groups = len(blocks)
    members = block * groups
    field = shape((members, channels, cells), bf16)
    spec = pl.BlockSpec((block, channels, cells), lambda d, place: (place[0] ^ d, 0, 0))
    sums = shape((members, HEADS * members), f32)
    operands = (*blocks, w_qkv, gain, lat)
    return pl.pallas_call(
        first_kernel,
        grid_spec=pltpu.PrefetchScalarGridSpec(
            num_scalar_prefetch=1,
            grid=(groups,),
            in_specs=[whole(t) for t in operands],
            out_specs=[spec] * 4 + [whole(sums)],
            scratch_shapes=[pltpu.VMEM(field.shape, bf16)] * 2,
        ),
        out_shape=[field] * 4 + [sums],
        compiler_params=params(),
    )(place, *operands)


def middle_call(divisor, block, sums, v_all, rows, cot, weights, gain):
    members, channels, cells = rows.shape
    w_out, w_up, w_down = weights
    inner = w_up.shape[0]
    spec = pl.BlockSpec((block, channels, cells), lambda step: (step, 0, 0))
    outs = [
        shape((members, channels, cells), bf16),
        shape((members, channels, cells), f32),
        shape((members, channels, cells), bf16),
        shape(sums.shape, f32),
        shape((inner, channels), f32),
        shape((inner, channels), f32),
        shape((channels, channels), f32),
        shape((channels, 1), f32),
    ]
    constants = (w_out, w_out.T, w_up, w_up.T, w_down, w_down.T, gain)
    return pl.pallas_call(
        functools.partial(middle_kernel, divisor),
        grid=(members // block,),
        in_specs=[whole(sums), whole(v_all), spec, spec] + [whole(t) for t in constants],
        out_specs=[spec] * 3 + [whole(t) for t in outs[3:]],
        scratch_shapes=[pltpu.VMEM((members, channels, cells), bf16)] * 2,
        out_shape=outs,
        compiler_params=params(),
    )(sums, v_all, rows, cot, *constants)


def last_call(divisor, block, sums, dots, q_all, k_all, grad_all, rows, resid, w_qkv, gain, lat):
    members, channels, cells = rows.shape
    spec = pl.BlockSpec((block, channels, cells), lambda step: (step, 0, 0))
    outs = [
        shape((members, channels, cells), bf16),
        shape(w_qkv.shape, f32),
        shape((channels, 1), f32),
    ]
    front = (sums, dots, q_all, k_all, grad_all)
    constants = (w_qkv.T, gain, lat)
    return pl.pallas_call(
        functools.partial(last_kernel, divisor),
        grid=(members // block,),
        in_specs=[whole(t) for t in front] + [spec, spec] + [whole(t) for t in constants],
        out_specs=[spec] + [whole(t) for t in outs[1:]],
        scratch_shapes=[pltpu.VMEM((members, 3 * channels, cells), bf16)],
        out_shape=outs,
        compiler_params=params(),
    )(*front, rows, resid, *constants)


def exchange(array, distance, axis="member"):
    size = lax.axis_size(axis)
    return lax.ppermute(array, axis, [(i, i ^ distance) for i in range(size)])


def member_sum(array):
    size = lax.axis_size("member")
    distance = 1
    while distance < size:
        array = array + exchange(array, distance)
        distance *= 2
    return array


def gather_sum(array):
    array = member_sum(array)
    size = lax.axis_size("grid")
    copies = jnp.broadcast_to(array[None], (size,) + array.shape)
    return jnp.sum(lax.all_to_all(copies, "grid", 0, 0), axis=0)


def scatter_sum(array):
    array = member_sum(array)
    size = lax.axis_size("grid")
    pieces = array.reshape(size, array.shape[0] // size, array.shape[1])
    own = jnp.sum(lax.all_to_all(pieces, "grid", 0, 0), axis=0)
    copies = jnp.broadcast_to(own[None], (size,) + own.shape)
    return lax.all_to_all(copies, "grid", 0, 0).reshape(array.shape)


def shards(fields, cotangent, w_query, w_key, w_value, w_out, w_up, w_down, gain_attn, gain_mlp):
    block, channels, tile = fields.shape
    groups = lax.axis_size("member")
    me = lax.axis_index("member")
    width = tile // groups
    divisor = sharpness_divisor / ((channels // HEADS) * tile * lax.axis_size("grid"))

    def outgoing(array, d):
        return lax.dynamic_slice_in_dim(array, (me ^ d) * width, width, axis=2)

    def incoming(array):
        return [outgoing(array, 0)] + [exchange(outgoing(array, d), d) for d in range(1, groups)]

    def outward(array):
        whole_tile = jnp.zeros((block, channels, tile), array.dtype)
        for d in range(groups):
            piece = lax.dynamic_slice_in_dim(array, (me ^ d) * block, block, axis=0)
            if d:
                piece = exchange(piece, d)
            whole_tile = lax.dynamic_update_slice_in_dim(whole_tile, piece, (me ^ d) * width, 2)
        return whole_tile

    position = (me * width).astype(f32) + jnp.arange(width, dtype=f32)
    lat = jnp.cos(lat_span * (position + 0.5) / tile)[None, :]
    w_qkv = jnp.concatenate([w_query, w_key, w_value], axis=0)
    gain_a, gain_m = gain_attn[:, None], gain_mlp[:, None]

    rows, q_all, k_all, v_all, sums = first_call(
        me[None].astype(jnp.int32), incoming(fields), w_qkv, gain_a, lat
    )
    pieces = incoming(cotangent)
    cot = jnp.zeros((block * groups, channels, width), bf16)
    for d, piece in enumerate(pieces):
        cot = lax.dynamic_update_slice_in_dim(cot, piece, (me ^ d) * block, 0)
    sums = gather_sum(sums)

    result, resid, grad_all, dots, g_up, g_down_t, g_out, g_gain_m = middle_call(
        divisor, block // 2, sums, v_all, rows, cot, (w_out, w_up, w_down), gain_m
    )
    result = outward(result)
    dots = gather_sum(dots)

    grad_rows, g_qkv, g_gain_a = last_call(
        divisor, block // 2, sums, dots, q_all, k_all, grad_all, rows, resid, w_qkv, gain_a, lat
    )
    grad_fields = outward(grad_rows)

    gains = jnp.pad(jnp.concatenate([g_gain_a, g_gain_m], axis=1), ((0, 0), (0, channels - 2)))
    left = jnp.concatenate([g_up, g_qkv], axis=0)
    right = jnp.concatenate([g_down_t, g_out, gains, jnp.zeros((channels, channels), f32)], axis=0)
    total = scatter_sum(jnp.concatenate([left, right], axis=1))
    inner = w_up.shape[0]
    left, right = total[:, :channels], total[:, channels:]
    g_up, g_qkv = left[:inner], left[inner:]
    g_down, g_out = right[:inner].T, right[inner : inner + channels]
    gains = right[inner + channels : inner + 2 * channels]
    return (
        result,
        grad_fields,
        g_qkv[:channels],
        g_qkv[channels : 2 * channels],
        g_qkv[2 * channels :],
        g_out,
        g_up,
        g_down,
        gains[:, 0],
        gains[:, 1],
    )


def solution(mesh):
    split = P("member", None, "grid")
    return jax.shard_map(
        shards,
        mesh=mesh,
        in_specs=(split, split) + (P(),) * 8,
        out_specs=(split, split) + (P(),) * 8,
        check_vma=False,
    )
```

time: 496 us -> 243 us (0.49)
  blocking collectives: 131 us -> 0 us
  matrix products: 90 us -> 0 us
  Pallas kernels: 0 us -> 72.8 us
  waiting for transfers between devices: 156 us -> 86.1 us
  local copies, waits for them, and re-layouts: 66.4 us -> 32.8 us
  starting transfers between devices: 21.3 us -> 41.2 us
  between operations: 14.9 us -> 1.07 us
  other arithmetic: 11.6 us -> 5.58 us
    psum x1 -> x0, waiting for transfers between devices: 138 us -> none  [shards(): summed = lax.psum(pack_sums(joined), ('member', 'grid'))]
    psum x2 -> x0, blocking collectives: 131 us -> none  [the longest x1 68.5 us: shards(): lax.psum(score_terms(query, key), ('member', 'grid')) * attention_divisor]
    dot_general x24 -> x0, matrix products: 90 us -> none  [the longest x6 26.8 us: project_back(): jnp.einsum('oc,mog->mcg', weight_matrix, grad, preferred_element_type=jnp...]
    pallas_call x0 -> x3, Pallas kernels: none -> 72.8 us  [the longest x1 42.6 us: middle_call(): pl.pallas_call(functools.partial(middle_kernel, divisor), grid=(members /...]
    ppermute x0 -> x18, waiting for transfers between devices: none -> 60.5 us  [exchange(): return lax.ppermute(array, axis, [(i, i ^ distance) for i in range(size)])]
    unnamed x48 -> x44, local copies, waits for them, and re-layouts: 40.6 us -> 3.93 us
    ppermute x0 -> x18, starting transfers between devices: none -> 19.4 us  [exchange(): return lax.ppermute(array, axis, [(i, i ^ distance) for i in range(size)])]
    all_to_all x3 -> x0, local copies, waits for them, and re-layouts: 11.9 us -> none  [the longest x1 5.45 us: shards(): lax.all_to_all(cotangent, 'member', split_axis=2, concat_axis=0, tiled=True)]
  transfers between devices with their start and end apart: 5 -> 22, of which waited for: 3 -> 11; matrix products, arithmetic and copies ran while one was open for 15% -> 13% of each run, Pallas kernels for 0% -> 13%
where the time goes in v1:
time: 243 us; the launch traced here: 240 us
  waiting for transfers between devices  86.1 us (35%)
  Pallas kernels  72.8 us (30%)
  starting transfers between devices  41.2 us (17%)
  local copies, waits for them, and re-layouts  32.8 us (13%)
  other arithmetic  5.58 us (2%)
    ppermute x18, waiting for transfers between devices, exchange(): return lax.ppermute(array, axis, [(i, i ^ distance) for i in range(size)])  60.5 us
    pallas_call x1, Pallas kernels, middle_call(): pl.pallas_call(functools.partial(middle_kernel, divisor), grid=(members /...  42.6 us
    ppermute x18, starting transfers between devices, exchange(): return lax.ppermute(array, axis, [(i, i ^ distance) for i in range(size)])  19.4 us
    pallas_call x1, Pallas kernels, last_call(): pl.pallas_call(functools.partial(last_kernel, divisor), grid=(members //...  19.1 us
    all_to_all x2, starting transfers between devices, gather_sum(): return jnp.sum(lax.all_to_all(copies, 'grid', 0, 0), axis=0)  14.1 us
    all_to_all x2, waiting for transfers between devices, gather_sum(): return jnp.sum(lax.all_to_all(copies, 'grid', 0, 0), axis=0)  11.7 us
    pallas_call x1, Pallas kernels, first_call(): pl.pallas_call(first_kernel, grid_spec=pltpu.PrefetchScalarGridSpec(num_s...  11.1 us
    dynamic_update_slice x6, local copies, waits for them, and re-layouts, outward(): lax.dynamic_update_slice_in_dim(whole_tile, piece, (me ^ d) * width, 2)  7.9 us
  transfers between devices with their start and end apart: 22, of which 11 were waited for; matrix products, arithmetic and copies ran while one was open for 13% of the time, Pallas kernels for 13%

profile of v1, /device:TPU:1, one launch (start us, length us, event | category | flops | bytes accessed | tf_op | source)
XLA Modules:
  0.0 239.6 jit_solution(14892652585046938083)
XLA Ops:
  0.7 2.9 %constant_dynamic-slice_fusion.9 = (bf16[8,64,512]{2,1,0:T(8,128)(2,1)}, bf16[8,64,512]{2,1,0:T(8,128)(2,1)}, bf16[8,64,512]{2,1,0:T(8,128)(2,1)}, bf16[8,64,512]{2,1,0:T(8,128)(2,1)}) fusion(bf16[8,64,2048]{2,1,0:T(8,128)(2,1)} %param.10, s32[]{:T(128)S(6)} %select_n.19, s32[]{:T(128)S(6)} %select_n.17, s32[]{:T(128)S(6)} %select_n.16, s32[]{:T(128)S(6)} %select_n.18), kind=kLoop, calls=%fused_computation.33 | loop fusion | bytes 4194320 | tf_op jit(solution)/shard_map/dynamic_slice | solution.py:395
  3.6 1.4 collective-permute-start
  5.0 1.7 collective-permute-start.1
  7.0 2.7 %constant_dynamic-slice_fusion.6 = (bf16[8,64,512]{2,1,0:T(8,128)(2,1)}, bf16[8,64,512]{2,1,0:T(8,128)(2,1)}, bf16[32,64,512]{2,1,0:T(8,128)(2,1)S(1)}, bf16[8,64,512]{2,1,0:T(8,128)(2,1)}) fusion(bf16[8,64,2048]{2,1,0:T(8,128)(2,1)} %param.11, s32[]{:T(128)S(6)} %select_n.19, s32[]{:T(128)S(6)} %select_n.17, bf16[32,64,512]{2,1,0:T(8,128)(2,1)S(1)} %broadcast_in_dim.37, ...), kind=kLoop, calls=%fused_computation.27 | loop fusion | bytes 4194324 | tf_op jit(solution)/shard_map/dynamic_slice | solution.py:395
  10.1 1.4 collective-permute-start.6
  14.4 4.9 %collective-permute-done.1.x2 = bf16[8,64,512]{2,1,0:T(8,128)(2,1)} collective-permute-done((bf16[8,64,512]{2,1,0:T(8,128)(2,1)}, bf16[8,64,512]{2,1,0:T(8,128)(2,1)}, u32[]{:S(2)}, u32[]{:S(2)}) %collective-permute-start.1) | collective-permute-done | bytes 524320 | tf_op jit(solution)/shard_map/ppermute | solution.py:359
  19.3 11.4 %collective-permute-done.2.x3 = bf16[8,64,512]{2,1,0:T(8,128)(2,1)} collective-permute-done((bf16[8,64,512]{2,1,0:T(8,128)(2,1)}, bf16[8,64,512]{2,1,0:T(8,128)(2,1)}, u32[]{:S(2)}, u32[]{:S(2)}) %collective-permute-start.2) | collective-permute-done | bytes 524320 | tf_op jit(solution)/shard_map/ppermute | solution.py:359
  30.6 11.1 %shard_map.177 = (bf16[32,64,512]{2,1,0:T(8,128)(2,1)}, bf16[32,64,512]{2,1,0:T(8,128)(2,1)}, bf16[32,64,512]{2,1,0:T(8,128)(2,1)}, bf16[32,64,512]{2,1,0:T(8,128)(2,1)}, f32[32,128]{1,0:T(8,128)}) custom-call(s32[1]{0:T(128)} %bitcast.place, bf16[8,64,512]{2,1,0:T(8,128)(2,1)} %get-tuple-element.108.x0, bf16[8,64,512]{2,1,0:T(8,128)(2,1)} %copy-done.6, ...), custom_call_target="tpu_custom_call" | custom-call | tf_op jit(solution)/shard_map/pallas_call | solution.py:295
  42.1 1.1 collective-permute-done.3
  43.9 1.6 collective-permute-start.4
  45.6 7.4 %collective-permute-done.4 = f32[32,128]{1,0:T(8,128)S(1)} collective-permute-done((f32[32,128]{1,0:T(8,128)S(1)}, f32[32,128]{1,0:T(8,128)S(1)}, u32[]{:S(2)}, u32[]{:S(2)}) %collective-permute-start.4) | collective-permute-done | bytes 16416 | tf_op jit(solution)/shard_map/ppermute | solution.py:359
  53.8 10.2 %all-to-all-start = ((f32[32,32,128]{2,1,0:T(8,128)}), f32[32,32,128]{2,1,0:T(8,128)S(1)}, u32[]{:S(2)}, u32[]{:S(2)}) async-start(f32[32,32,128]{2,1,0:T(8,128)} %broadcast_in_dim.36), calls=%async_computation | async-start | bytes 1048576 | tf_op jit(solution)/shard_map/all_to_all | solution.py:375
  69.2 6.7 %all-to-all-done = f32[32,32,128]{2,1,0:T(8,128)S(1)} async-done(((f32[32,32,128]{2,1,0:T(8,128)}), f32[32,32,128]{2,1,0:T(8,128)S(1)}, u32[]{:S(2)}, u32[]{:S(2)}) %all-to-all-start) | async-done | bytes 524320 | tf_op jit(solution)/shard_map/all_to_all | solution.py:375
  76.6 42.6 %shard_map.178 = (bf16[32,64,512]{2,1,0:T(8,128)(2,1)}, f32[32,64,512]{2,1,0:T(8,128)}, bf16[32,64,512]{2,1,0:T(8,128)(2,1)}, f32[32,128]{1,0:T(8,128)}, f32[256...) custom-call(f32[32,128]{1,0:T(8,128)} %reduce_sum.27.sums, ...), custom_call_target="tpu_custom_call" | custom-call | tf_op jit(solution)/shard_map/pallas_call | solution.py:325
  119.2 2.5 %collective-permute-start.11 = (f32[32,128]{1,0:T(8,128)}, f32[32,128]{1,0:T(8,128)S(1)}, u32[]{:S(2)}, u32[]{:S(2)}) collective-permute-start(f32[32,128]{1,0:T(8,128)} %get-tuple-element.30), channel_id=1, source_target_pairs={{0,32},{32,0},{64,96},{96,64},{1,33},{33,1},{65,97},{97,65},{2,34}... | collective-permute-start | bytes 49160 | tf_op jit(solution)/shard_map/ppermute | solution.py:359
  124.2 1.8 collective-permute-done.12
  126.9 3.9 %all-to-all-start.1 = ((f32[32,32,128]{2,1,0:T(8,128)}), f32[32,32,128]{2,1,0:T(8,128)S(1)}, u32[]{:S(2)}, u32[]{:S(2)}) async-start(f32[32,32,128]{2,1,0:T(8,128)} %broadcast_in_dim.39), calls=%async_computation.1 | async-start | bytes 1048576 | tf_op jit(solution)/shard_map/all_to_all | solution.py:375
  132.4 1.6 broadcast.32.clone
  133.9 1.4 constant_dynamic-slice_fusion.2
  135.3 1.5 collective-permute-start.8
  137.5 5.0 %all-to-all-done.1 = f32[32,32,128]{2,1,0:T(8,128)S(1)} async-done(((f32[32,32,128]{2,1,0:T(8,128)}), f32[32,32,128]{2,1,0:T(8,128)S(1)}, u32[]{:S(2)}, u32[]{:S(2)}) %all-to-all-start.1) | async-done | bytes 524320 | tf_op jit(solution)/shard_map/all_to_all | solution.py:375
  143.2 19.1 %shard_map.179 = (bf16[32,64,512]{2,1,0:T(8,128)(2,1)}, f32[192,64]{1,0:T(8,128)}, f32[64,1]{1,0:T(8,128)}) custom-call(f32[32,128]{1,0:T(8,128)} %reduce_sum.27.sums, f32[32,128]{1,0:T(8,128)} %reduce_sum.28.dots, bf16[32,64,512]{2,1,0:T(8,128)(2,1)} %get-tuple-element.31.q_all, bf16[32,64,512]{2,1,0:T(8,128)(2,1)} %get-tuple-element.32.k_all, ...), custom_call_target="tpu_custom_call" | custom-call | tf_op jit(solution)/shard_map/pallas_call | solution.py:346
  163.3 1.2 fusion.1
  164.5 2.9 %collective-permute-start.16 = (f32[448,128]{1,0:T(8,128)S(1)}, f32[448,128]{1,0:T(8,128)S(1)}, u32[]{:S(2)}, u32[]{:S(2)}) collective-permute-start(f32[448,128]{1,0:T(8,128)S(1)} %fusion.1), channel_id=1, source_target_pairs={{0,32},{32,0},{64,96},{96,64},{1,33},{33,1},{65,97},{97,65},{2,34}... | collective-permute-start | bytes 688136 | tf_op jit(solution)/shard_map/ppermute | solution.py:359
  168.4 1.2 constant_dynamic-slice_fusion.5
  173.5 1.9 constant_dynamic-update-slice_fusion.3
  175.4 32.8 %collective-permute-done.17 = f32[448,128]{1,0:T(8,128)S(1)} collective-permute-done((f32[448,128]{1,0:T(8,128)S(1)}, f32[448,128]{1,0:T(8,128)S(1)}, u32[]{:S(2)}, u32[]{:S(2)}) %collective-permute-start.17) | collective-permute-done | bytes 229408 | tf_op jit(solution)/shard_map/ppermute | solution.py:359
  208.9 3.9 %all-to-all-start.2 = ((f32[32,14,128]{2,1,0:T(8,128)}), f32[32,14,128]{2,1,0:T(8,128)S(1)}, u32[]{:S(2)}, u32[]{:S(2)}) async-start(f32[32,14,128]{2,1,0:T(8,128)} %reshape.45), calls=%async_computation.2 | async-start | bytes 524288 | tf_op jit(solution)/shard_map/all_to_all | solution.py:382
  212.8 1.9 constant_dynamic-update-slice_fusion.2
  215.8 6.6 %all-to-all-done.2 = f32[32,14,128]{2,1,0:T(8,128)S(1)} async-done(((f32[32,14,128]{2,1,0:T(8,128)}), f32[32,14,128]{2,1,0:T(8,128)S(1)}, u32[]{:S(2)}, u32[]{:S(2)}) %all-to-all-start.2) | async-done | bytes 229408 | tf_op jit(solution)/shard_map/all_to_all | solution.py:382
  223.1 3.9 %all-to-all-start.3 = ((f32[32,14,128]{2,1,0:T(8,128)}), f32[32,14,128]{2,1,0:T(8,128)S(1)}, u32[]{:S(2)}, u32[]{:S(2)}) async-start(f32[32,14,128]{2,1,0:T(8,128)} %broadcast_in_dim.41), calls=%async_computation.3 | async-start | bytes 524288 | tf_op jit(solution)/shard_map/all_to_all | solution.py:384
  229.3 7.4 %all-to-all-done.3 = f32[32,14,128]{2,1,0:T(8,128)S(1)} async-done(((f32[32,14,128]{2,1,0:T(8,128)}), f32[32,14,128]{2,1,0:T(8,128)S(1)}, u32[]{:S(2)}, u32[]{:S(2)}) %all-to-all-start.3) | async-done | bytes 229408 | tf_op jit(solution)/shard_map/all_to_all | solution.py:384
  (104 shorter events, 31.0 us)
Async XLA Ops:
  3.6 9.9 %collective-permute-start = (bf16[8,64,512]{2,1,0:T(8,128)(2,1)}, bf16[8,64,512]{2,1,0:T(8,128)(2,1)S(1)}, u32[]{:S(2)}, u32[]{:S(2)}) collective-permute-start(bf16[8,64,512]{2,1,0:T(8,128)(2,1)} %get-tuple-element.107), channel_id=1, source_target_pairs={{0,32},{32,0},{64,96},{96,64},{1,33},{33,1},{65,97},{97,65},{2,34}... | collective-permute-start | bytes 1572872 | tf_op jit(solution)/shard_map/ppermute | solution.py:359
  5.0 14.3 %collective-permute-start.1 = (bf16[8,64,512]{2,1,0:T(8,128)(2,1)}, bf16[8,64,512]{2,1,0:T(8,128)(2,1)}, u32[]{:S(2)}, u32[]{:S(2)}) collective-permute-start(bf16[8,64,512]{2,1,0:T(8,128)(2,1)} %get-tuple-element.109), channel_id=1, source_target_pairs={{0,64},{32,96},{64,0},{96,32},{1,65},{33,97},{65,1},{97,33},{2,66}... | collective-permute-start | bytes 1572872 | tf_op jit(solution)/shard_map/ppermute | solution.py:359
  6.7 23.9 %collective-permute-start.2 = (bf16[8,64,512]{2,1,0:T(8,128)(2,1)}, bf16[8,64,512]{2,1,0:T(8,128)(2,1)}, u32[]{:S(2)}, u32[]{:S(2)}) collective-permute-start(bf16[8,64,512]{2,1,0:T(8,128)(2,1)} %get-tuple-element.106), channel_id=1, source_target_pairs={{0,96},{32,64},{64,32},{96,0},{1,97},{33,65},{65,33},{97,1},{2,98}... | collective-permute-start | bytes 1572872 | tf_op jit(solution)/shard_map/ppermute | solution.py:359
  9.7 57.2 %collective-permute-start.5 = (bf16[8,64,512]{2,1,0:T(8,128)(2,1)}, bf16[8,64,512]{2,1,0:T(8,128)(2,1)}, u32[]{:S(2)}, u32[]{:S(2)}) collective-permute-start(bf16[8,64,512]{2,1,0:T(8,128)(2,1)} %get-tuple-element.103), channel_id=1, source_target_pairs={{0,32},{32,0},{64,96},{96,64},{1,33},{33,1},{65,97},{97,65},{2,34}... | collective-permute-start | bytes 1572872 | tf_op jit(solution)/shard_map/ppermute | solution.py:359
  10.1 57.9 %collective-permute-start.6 = (bf16[8,64,512]{2,1,0:T(8,128)(2,1)}, bf16[8,64,512]{2,1,0:T(8,128)(2,1)S(1)}, u32[]{:S(2)}, u32[]{:S(2)}) collective-permute-start(bf16[8,64,512]{2,1,0:T(8,128)(2,1)} %get-tuple-element.105), channel_id=1, source_target_pairs={{0,64},{32,96},{64,0},{96,32},{1,65},{33,97},{65,1},{97,33},{2,66}... | collective-permute-start | bytes 1572872 | tf_op jit(solution)/shard_map/ppermute | solution.py:359
  11.6 52.5 %copy-start.10 = (bf16[64,256]{1,0:T(8,128)(2,1)S(1)}, bf16[64,256]{1,0:T(8,128)(2,1)}, u32[]{:S(2)}) copy-start(bf16[64,256]{1,0:T(8,128)(2,1)} %w_down.1) | copy-start | bytes 98308
  11.9 52.9 %copy-start.9 = (bf16[256,64]{0,1:T(8,128)(2,1)S(1)}, bf16[256,64]{0,1:T(8,128)(2,1)}, u32[]{:S(2)}) copy-start(bf16[256,64]{0,1:T(8,128)(2,1)} %param.16) | copy-start | bytes 98308
  12.0 53.5 %copy-start.17 = (f32[64]{0:T(128)S(1)}, f32[64]{0:T(128)}, u32[]{:S(2)}) copy-start(f32[64]{0:T(128)} %param.19) | copy-start | bytes 772
  12.7 53.5 %copy-start.12 = (bf16[64,64]{1,0:T(8,128)(2,1)S(1)}, bf16[64,64]{1,0:T(8,128)(2,1)}, u32[]{:S(2)}) copy-start(bf16[64,64]{1,0:T(8,128)(2,1)} %w_out.1) | copy-start | bytes 24580
  13.4 17.2 %copy-start.6 = (bf16[8,64,512]{2,1,0:T(8,128)(2,1)}, bf16[8,64,512]{2,1,0:T(8,128)(2,1)S(1)}, u32[]{:S(2)}) copy-start(bf16[8,64,512]{2,1,0:T(8,128)(2,1)S(1)} %collective-permute-done.x1) | copy-start | bytes 1572868
  13.4 54.7 %collective-permute-start.7 = (bf16[8,64,512]{2,1,0:T(8,128)(2,1)}, bf16[8,64,512]{2,1,0:T(8,128)(2,1)}, u32[]{:S(2)}, u32[]{:S(2)}) collective-permute-start(bf16[8,64,512]{2,1,0:T(8,128)(2,1)} %get-tuple-element.102), channel_id=1, source_target_pairs={{0,96},{32,64},{64,32},{96,0},{1,97},{33,65},{65,33},{97,1},{2,98}... | collective-permute-start | bytes 1572872 | tf_op jit(solution)/shard_map/ppermute | solution.py:359
  41.7 1.5 collective-permute-start.3
  43.9 9.1 %collective-permute-start.4 = (f32[32,128]{1,0:T(8,128)S(1)}, f32[32,128]{1,0:T(8,128)S(1)}, u32[]{:S(2)}, u32[]{:S(2)}) collective-permute-start(f32[32,128]{1,0:T(8,128)S(1)} %add.98), channel_id=1, source_target_pairs={{0,64},{32,96},{64,0},{96,32},{1,65},{33,97},{65,1},{97,33},{2,66}... | collective-permute-start | bytes 49160 | tf_op jit(solution)/shard_map/ppermute | solution.py:359
  53.8 22.1 %all-to-all-start = ((f32[32,32,128]{2,1,0:T(8,128)}), f32[32,32,128]{2,1,0:T(8,128)S(1)}, u32[]{:S(2)}, u32[]{:S(2)}) async-start(f32[32,32,128]{2,1,0:T(8,128)} %broadcast_in_dim.36), calls=%async_computation | async-start | bytes 1048576 | tf_op jit(solution)/shard_map/all_to_all | solution.py:375
  119.2 14.8 %copy-start.2 = (bf16[32,64,512]{2,1,0:T(8,128)(2,1)S(1)}, bf16[32,64,512]{2,1,0:T(8,128)(2,1)}, u32[]{:S(2)}) copy-start(bf16[32,64,512]{2,1,0:T(8,128)(2,1)} %get-tuple-element.29) | copy-start | bytes 6291460
  119.2 3.6 %collective-permute-start.11 = (f32[32,128]{1,0:T(8,128)}, f32[32,128]{1,0:T(8,128)S(1)}, u32[]{:S(2)}, u32[]{:S(2)}) collective-permute-start(f32[32,128]{1,0:T(8,128)} %get-tuple-element.30), channel_id=1, source_target_pairs={{0,32},{32,0},{64,96},{96,64},{1,33},{33,1},{65,97},{97,65},{2,34}... | collective-permute-start | bytes 49160 | tf_op jit(solution)/shard_map/ppermute | solution.py:359
  123.5 2.6 %collective-permute-start.12 = (f32[32,128]{1,0:T(8,128)S(1)}, f32[32,128]{1,0:T(8,128)S(1)}, u32[]{:S(2)}, u32[]{:S(2)}) collective-permute-start(f32[32,128]{1,0:T(8,128)S(1)} %add.104), channel_id=1, source_target_pairs={{0,64},{32,96},{64,0},{96,32},{1,65},{33,97},{65,1},{97,33},{2,66}... | collective-permute-start | bytes 49160 | tf_op jit(solution)/shard_map/ppermute | solution.py:359
  126.9 15.6 %all-to-all-start.1 = ((f32[32,32,128]{2,1,0:T(8,128)}), f32[32,32,128]{2,1,0:T(8,128)S(1)}, u32[]{:S(2)}, u32[]{:S(2)}) async-start(f32[32,32,128]{2,1,0:T(8,128)} %broadcast_in_dim.39), calls=%async_computation.1 | async-start | bytes 1048576 | tf_op jit(solution)/shard_map/all_to_all | solution.py:375
  135.3 35.6 %collective-permute-start.8 = (bf16[8,64,512]{2,1,0:T(8,128)(2,1)}, bf16[8,64,512]{2,1,0:T(8,128)(2,1)S(1)}, u32[]{:S(2)}, u32[]{:S(2)}) collective-permute-start(bf16[8,64,512]{2,1,0:T(8,128)(2,1)} %get-tuple-element.100), channel_id=1, source_target_pairs={{0,32},{32,0},{64,96},{96,64},{1,33},{33,1},{65,97},{97,65},{2,34}... | collective-permute-start | bytes 1572872 | tf_op jit(solution)/shard_map/ppermute | solution.py:359
  136.8 35.1 %collective-permute-start.9 = (bf16[8,64,512]{2,1,0:T(8,128)(2,1)}, bf16[8,64,512]{2,1,0:T(8,128)(2,1)}, u32[]{:S(2)}, u32[]{:S(2)}) collective-permute-start(bf16[8,64,512]{2,1,0:T(8,128)(2,1)} %get-tuple-element.99), channel_id=1, source_target_pairs={{0,64},{32,96},{64,0},{96,32},{1,65},{33,97},{65,1},{97,33},{2,66}... | collective-permute-start | bytes 1572872 | tf_op jit(solution)/shard_map/ppermute | solution.py:359
  143.2 20.1 %copy-start.4 = (f32[256,64]{1,0:T(8,128)S(1)}, f32[256,64]{1,0:T(8,128)}, u32[]{:S(2)}) copy-start(f32[256,64]{1,0:T(8,128)} %get-tuple-element.36) | copy-start | bytes 196612
  143.2 20.1 %copy-start.5 = (f32[256,64]{1,0:T(8,128)S(1)}, f32[256,64]{1,0:T(8,128)}, u32[]{:S(2)}) copy-start(f32[256,64]{1,0:T(8,128)} %get-tuple-element.38) | copy-start | bytes 196612
  143.2 20.1 %copy-start.11 = (f32[64,64]{1,0:T(8,128)S(1)}, f32[64,64]{1,0:T(8,128)}, u32[]{:S(2)}) copy-start(f32[64,64]{1,0:T(8,128)} %get-tuple-element.39) | copy-start | bytes 49156
  143.2 24.2 %copy-start.7 = (bf16[8,64,512]{2,1,0:T(8,128)(2,1)S(1)}, bf16[8,64,512]{2,1,0:T(8,128)(2,1)}, u32[]{:S(2)}) copy-start(bf16[8,64,512]{2,1,0:T(8,128)(2,1)} %get-tuple-element.98) | copy-start | bytes 1572868
  164.5 5.5 %collective-permute-start.16 = (f32[448,128]{1,0:T(8,128)S(1)}, f32[448,128]{1,0:T(8,128)S(1)}, u32[]{:S(2)}, u32[]{:S(2)}) collective-permute-start(f32[448,128]{1,0:T(8,128)S(1)} %fusion.1), channel_id=1, source_target_pairs={{0,32},{32,0},{64,96},{96,64},{1,33},{33,1},{65,97},{97,65},{2,34}... | collective-permute-start | bytes 688136 | tf_op jit(solution)/shard_map/ppermute | solution.py:359
  167.4 45.4 %collective-permute-start.10 = (bf16[8,64,512]{2,1,0:T(8,128)(2,1)S(1)}, bf16[8,64,512]{2,1,0:T(8,128)(2,1)}, u32[]{:S(2)}, u32[]{:S(2)}) collective-permute-start(bf16[8,64,512]{2,1,0:T(8,128)(2,1)S(1)} %copy-done.7), channel_id=1, source_target_pairs={{0,96},{32,64},{64,32},{96,0},{1,97},{33,65},{65,33},{97,1},{2,98}... | collective-permute-start | bytes 1572872 | tf_op jit(solution)/shard_map/ppermute | solution.py:359
  169.5 45.1 %collective-permute-start.13 = (bf16[8,64,512]{2,1,0:T(8,128)(2,1)}, bf16[8,64,512]{2,1,0:T(8,128)(2,1)}, u32[]{:S(2)}, u32[]{:S(2)}) collective-permute-start(bf16[8,64,512]{2,1,0:T(8,128)(2,1)} %get-tuple-element.96), channel_id=1, source_target_pairs={{0,32},{32,0},{64,96},{96,64},{1,33},{33,1},{65,97},{97,65},{2,34}... | collective-permute-start | bytes 1572872 | tf_op jit(solution)/shard_map/ppermute | solution.py:359
  170.0 57.0 %collective-permute-start.14 = (bf16[8,64,512]{2,1,0:T(8,128)(2,1)}, bf16[8,64,512]{2,1,0:T(8,128)(2,1)}, u32[]{:S(2)}, u32[]{:S(2)}) collective-permute-start(bf16[8,64,512]{2,1,0:T(8,128)(2,1)} %get-tuple-element.95), channel_id=1, source_target_pairs={{0,64},{32,96},{64,0},{96,32},{1,65},{33,97},{65,1},{97,33},{2,66}... | collective-permute-start | bytes 1572872 | tf_op jit(solution)/shard_map/ppermute | solution.py:359
  170.9 57.3 %collective-permute-start.15 = (bf16[8,64,512]{2,1,0:T(8,128)(2,1)}, bf16[8,64,512]{2,1,0:T(8,128)(2,1)}, u32[]{:S(2)}, u32[]{:S(2)}) collective-permute-start(bf16[8,64,512]{2,1,0:T(8,128)(2,1)} %get-tuple-element.94), channel_id=1, source_target_pairs={{0,96},{32,64},{64,32},{96,0},{1,97},{33,65},{65,33},{97,1},{2,98}... | collective-permute-start | bytes 1572872 | tf_op jit(solution)/shard_map/ppermute | solution.py:359
  171.9 36.2 %collective-permute-start.17 = (f32[448,128]{1,0:T(8,128)S(1)}, f32[448,128]{1,0:T(8,128)S(1)}, u32[]{:S(2)}, u32[]{:S(2)}) collective-permute-start(f32[448,128]{1,0:T(8,128)S(1)} %fusion.5), channel_id=1, source_target_pairs={{0,64},{32,96},{64,0},{96,32},{1,65},{33,97},{65,1},{97,33},{2,66}... | collective-permute-start | bytes 688136 | tf_op jit(solution)/shard_map/ppermute | solution.py:359
  208.9 13.5 %all-to-all-start.2 = ((f32[32,14,128]{2,1,0:T(8,128)}), f32[32,14,128]{2,1,0:T(8,128)S(1)}, u32[]{:S(2)}, u32[]{:S(2)}) async-start(f32[32,14,128]{2,1,0:T(8,128)} %reshape.45), calls=%async_computation.2 | async-start | bytes 524288 | tf_op jit(solution)/shard_map/all_to_all | solution.py:382
  223.1 13.5 %all-to-all-start.3 = ((f32[32,14,128]{2,1,0:T(8,128)}), f32[32,14,128]{2,1,0:T(8,128)S(1)}, u32[]{:S(2)}, u32[]{:S(2)}) async-start(f32[32,14,128]{2,1,0:T(8,128)} %broadcast_in_dim.41), calls=%async_computation.3 | async-start | bytes 524288 | tf_op jit(solution)/shard_map/all_to_all | solution.py:384
  (8 other events, 45.0 us)

commit v2 on v0

v2 whole, which is shorter than its diff:
```python
import functools

import jax
import jax.numpy as jnp
from jax import lax
from jax.experimental import pallas as pl
from jax.experimental.pallas import tpu as pltpu
from jax.sharding import PartitionSpec as P

HEADS = 4

norm_eps = 1e-05
lat_span = 1.4
sharpness_divisor = 32.0

VMEM_LIMIT = 40 * 1024 * 1024
UNROLL = 4
Z_PARTS = 2
f32 = jnp.float32
bf16 = jnp.bfloat16


def dot(left, right):
    return lax.dot_general(left, right, (((1,), (0,)), ((), ())), preferred_element_type=f32)


def dot_t(left, right):
    return lax.dot_general(left, right, (((1,), (1,)), ((), ())), preferred_element_type=f32)


def channel_hat(values):
    center = values - jnp.mean(values, axis=0, keepdims=True)
    spread = lax.rsqrt(jnp.mean(center * center, axis=0, keepdims=True) + norm_eps)
    return center * spread, spread


def norm_back(scaled, hat, spread):
    return spread * (
        scaled
        - jnp.mean(scaled, axis=0, keepdims=True)
        - hat * jnp.mean(scaled * hat, axis=0, keepdims=True)
    )


def member_rows(members, part):
    shape = (members * part, members)
    row = lax.broadcasted_iota(jnp.int32, shape, 0)
    column = lax.broadcasted_iota(jnp.int32, shape, 1)
    return lax.div(row, part) == column


def same_channel(members, part):
    shape = (members * part, members * part)
    row = lax.broadcasted_iota(jnp.int32, shape, 0)
    column = lax.broadcasted_iota(jnp.int32, shape, 1)
    return lax.rem(row, part) == lax.rem(column, part)


def head_rows(ref, head, part):
    members, _, cells = ref.shape
    return ref[:, head * part : (head + 1) * part, :].reshape(members * part, cells)


def pair_sums(left_ref, right_ref, out_ref):
    members, channels, _ = left_ref.shape
    part = channels // HEADS
    same = same_channel(members, part)
    collect = member_rows(members, part).astype(f32)
    sums = []
    for head in range(HEADS):
        pairs = dot_t(head_rows(left_ref, head, part), head_rows(right_ref, head, part))
        pairs = jnp.where(same, pairs, 0.0).reshape(members, part, members * part)
        lanes = jnp.sum(pairs, axis=1)
        sums.append(
            lax.dot_general(
                lanes,
                collect,
                (((1,), (0,)), ((), ())),
                precision=lax.Precision.HIGHEST,
                preferred_element_type=f32,
            )
        )
    out_ref[...] = jnp.concatenate(sums, axis=1)


def softmax_probs(score_sums, head, divisor):
    members = score_sums.shape[0]
    expo = jnp.exp(score_sums[:, head * members : (head + 1) * members] * divisor)
    return expo / jnp.sum(expo, axis=1, keepdims=True)


def per_channel(weights, spread, same, transposed):
    rows = (dot_t if transposed else dot)(spread, weights).astype(bf16)
    return jnp.where(same, dot_t(rows, spread), 0.0).astype(bf16)


def loop(count, body):
    def step(i, carry):
        body(i)
        return carry

    lax.fori_loop(0, count, step, 0, unroll=UNROLL)


def start(copies):
    for copy in copies:
        copy.start()
    return copies


def wait(copies):
    for copy in copies:
        copy.wait()


def own_cells(place, ref, width):
    return ref.at[:, :, pl.ds(pl.multiple_of(place[0] * width, width), width)]


def first_kernel(
    place, fields, x1, x2, x3, w_qkv, gain, lat, q_out, k_out, v_out, sums, x, q_all, k_all, v_all, sin, sout
):
    groups, block, channels, cells = x.shape
    sources = (own_cells(place, fields, cells), x1, x2, x3)
    arrive = start(
        [pltpu.make_async_copy(t, x.at[d], sin.at[d]) for d, t in enumerate(sources)]
    )
    leave = []
    for d in range(groups):
        base = (place[0] ^ d) * block
        arrive[d].wait()

        def member(i, base=base, d=d):
            hat, _ = channel_hat(x[d, i].astype(f32))
            normed = (hat * gain[...]).astype(bf16)
            qkv = dot(w_qkv[...], normed)
            q_all[base + i] = (qkv[:channels] * lat[...]).astype(bf16)
            k_all[base + i] = qkv[channels : 2 * channels].astype(bf16)
            v_all[base + i] = qkv[2 * channels :].astype(bf16)

        loop(block, member)
        for n, (here, there) in enumerate(((q_all, q_out), (k_all, k_out), (v_all, v_out))):
            at = pl.ds(base, block)
            leave += start([pltpu.make_async_copy(here.at[at], there.at[at], sout.at[n, d])])
    pair_sums(q_all, k_all, sums)
    wait(leave)


def later_half(mixed, raw, grads_in, weights, result, resid_out, mixed_grad, grads):
    w_out, w_out_t, w_up, w_up_t, w_down, w_down_t, gain = weights
    g_up, g_down, g_out, g_gain = grads
    resid = raw.astype(f32) + dot(w_out[...], mixed)
    hat, spread = channel_hat(resid)
    normed = (hat * gain[...]).astype(bf16)
    inner = dot(w_up[...], normed)
    sig = 0.5 * jnp.tanh(0.5 * inner) + 0.5
    hidden = (inner * sig).astype(bf16)
    result[...] = (resid + dot(w_down[...], hidden)).astype(bf16)
    grad_inner = (
        dot(w_down_t[...], grads_in) * (sig * (1.0 + inner * (1.0 - sig)))
    ).astype(bf16)
    grad_normed = dot(w_up_t[...], grad_inner)
    grad_resid = grads_in.astype(f32) + norm_back(grad_normed * gain[...], hat, spread)
    resid_out[...] = grad_resid
    grad_resid_b = grad_resid.astype(bf16)
    mixed_grad[...] = dot(w_out_t[...], grad_resid_b).astype(bf16)
    g_up[...] += dot_t(grad_inner, normed)
    g_down[...] += dot_t(hidden, grads_in)
    g_out[...] += dot_t(grad_resid_b, mixed)
    g_gain[...] += jnp.sum(grad_normed * hat, axis=1, keepdims=True)


def far_kernel(divisor, *refs):
    place, sums, more_sums, v_hbm, x2, x3, c2, c3 = refs[:8]
    weights, refs = refs[8:15], refs[15:]
    outs, near_out, grads, refs = refs[:4], refs[4], refs[5:9], refs[9:]
    v_all, mixed_all, x, c, result, resid, grad, sin, sout = refs
    members, channels, cells = v_all.shape
    block = members // 4
    part = channels // HEADS
    arrive = start(
        [
            pltpu.make_async_copy(here, there, sin.at[n])
            for n, (here, there) in enumerate(
                ((v_hbm, v_all), (x2, x.at[0]), (c2, c.at[0]), (x3, x.at[1]), (c3, c.at[1]))
            )
        ]
    )
    for ref in grads:
        ref[...] = jnp.zeros_like(ref)
    spread = member_rows(members, part).astype(bf16)
    same = same_channel(members, part)
    score_sums = sums[...] + more_sums[...]
    arrive[0].wait()
    for head in range(HEADS):
        probs = softmax_probs(score_sums, head, divisor).astype(bf16)
        matrix = per_channel(probs, spread, same, False)
        mixed = dot(matrix, head_rows(v_all, head, part)).astype(bf16)
        mixed_all[:, head * part : (head + 1) * part, :] = mixed.reshape(members, part, cells)
    leave = start(
        [
            pltpu.make_async_copy(
                mixed_all.at[pl.ds((place[0] ^ d) * block, block)], near_out.at[d], sout.at[d]
            )
            for d in range(2)
        ]
    )
    for n in range(2):
        base = (place[0] ^ (2 + n)) * block
        wait(arrive[1 + 2 * n : 3 + 2 * n])

        def member(i, base=base, n=n):
            later_half(
                mixed_all[base + i],
                x[n, i],
                c[n, i],
                weights,
                result.at[n, i],
                resid.at[n, i],
                grad.at[n, i],
                grads,
            )

        loop(block, member)
        leave += start(
            [
                pltpu.make_async_copy(result.at[n], outs[n], sout.at[2 + n]),
                pltpu.make_async_copy(resid.at[n], outs[2].at[n], sout.at[4 + n]),
                pltpu.make_async_copy(grad.at[n], outs[3].at[n], sout.at[6 + n]),
            ]
        )
    wait(leave)


def near_kernel(*refs):
    place, v_hbm, fields, x1, cotangent, c1, near, far_grad = refs[:8]
    weights, begun, refs = refs[8:15], refs[15:19], refs[19:]
    outs, (own, other), refs = refs[:4], refs[4:6], refs[6:]
    v_all, grad_all, mixed, x, c, result, resid, g_up, g_down, g_out, g_gain, early, sin, sout = refs
    grads = (g_up, g_down, g_out, g_gain)
    members, channels, cells = v_all.shape
    block = members // 4
    arrive = start(
        [
            pltpu.make_async_copy(here, there, sin.at[n])
            for n, (here, there) in enumerate(
                (
                    (near, mixed),
                    (own_cells(place, fields, cells), x.at[0]),
                    (own_cells(place, cotangent, cells), c.at[0]),
                    (x1, x.at[1]),
                    (c1, c.at[1]),
                    (v_hbm, v_all),
                    (far_grad.at[0], grad_all.at[pl.ds((place[0] ^ 2) * block, block)]),
                    (far_grad.at[1], grad_all.at[pl.ds((place[0] ^ 3) * block, block)]),
                )
            )
        ]
    )
    for ref, value in zip(grads, begun):
        ref[...] = value[...]
    arrive[0].wait()
    leave = []
    for n in range(2):
        base = (place[0] ^ n) * block
        wait(arrive[1 + 2 * n : 3 + 2 * n])

        def member(i, base=base, n=n):
            later_half(
                mixed[n, i],
                x[n, i],
                c[n, i],
                weights,
                result.at[n, i],
                resid.at[n, i],
                grad_all.at[base + i],
                grads,
            )

        loop(block, member)
        leave += start(
            [
                pltpu.make_async_copy(result.at[n], outs[n], sout.at[n]),
                pltpu.make_async_copy(resid.at[n], outs[2].at[n], sout.at[2 + n]),
                pltpu.make_async_copy(
                    grad_all.at[pl.ds(base, block)], outs[3].at[n], sout.at[4 + n]
                ),
            ]
        )
    wait(arrive[5:])
    pair_sums(grad_all, v_all, own.at[:members])
    inner = g_up.shape[0]
    early[:inner, :channels] = g_up[...]
    early[:inner, channels:] = g_down[...]
    early[inner:, :channels] = g_out[...]
    early[inner:, channels:] = jnp.broadcast_to(g_gain[...], g_out.shape)
    half = early.shape[0] // 2
    core = lax.rem(place[0], 2)
    other[:members] = own[:members]
    own[members:] = early[pl.ds(pl.multiple_of(core * half, 8), half), :]
    other[members:] = early[pl.ds(pl.multiple_of((1 - core) * half, 8), half), :]
    wait(leave)


def last_kernel(divisor, *refs):
    place, sums, more_sums, dots, more_dots, q_hbm, k_hbm, near_grad, far_grad = refs[:9]
    fields, x1, x2, x3, near_resid, far_resid, w_qkv_t, gain, lat = refs[9:18]
    rows_out, own, other, refs = refs[18:22], refs[22], refs[23], refs[24:]
    q_all, k_all, grad_all, x, resid, rows, qkv_all, g_qkv, g_gain, late, sin, sout = refs
    members, channels, cells = q_all.shape
    part = channels // HEADS
    block = members // 4
    moves = [(k_hbm, k_all), (q_hbm, q_all)]
    for d in range(4):
        source = (near_grad if d < 2 else far_grad).at[d % 2]
        moves.append((source, grad_all.at[pl.ds((place[0] ^ d) * block, block)]))
    for d, source in ((2, x2), (3, x3), (1, x1), (0, own_cells(place, fields, cells))):
        moves.append((source, x.at[d]))
        moves.append(((near_resid if d < 2 else far_resid).at[d % 2], resid.at[d]))
    arrive = start(
        [pltpu.make_async_copy(here, there, sin.at[n]) for n, (here, there) in enumerate(moves)]
    )
    g_qkv[...] = jnp.zeros_like(g_qkv)
    g_gain[...] = jnp.zeros_like(g_gain)
    spread = member_rows(members, part).astype(bf16)
    same = same_channel(members, part)
    score_sums = sums[...] + more_sums[...]
    dot_sums = dots[:members] + more_dots[:members]
    probs, grad_scores = [], []
    for head in range(HEADS):
        prob = softmax_probs(score_sums, head, divisor)
        one = dot_sums[:, head * members : (head + 1) * members]
        grad_scores.append(
            (divisor * prob * (one - jnp.sum(prob * one, axis=1, keepdims=True))).astype(bf16)
        )
        probs.append(prob.astype(bf16))

    def put(offset, head, value):
        begin = offset + head * part
        qkv_all[:, begin : begin + part, :] = value.astype(bf16).reshape(members, part, cells)

    arrive[0].wait()
    for head in range(HEADS):
        matrix = per_channel(grad_scores[head], spread, same, False)
        put(0, head, dot(matrix, head_rows(k_all, head, part)) * lat[...])
    arrive[1].wait()
    for head in range(HEADS):
        matrix = per_channel(grad_scores[head], spread, same, True)
        put(channels, head, dot(matrix, head_rows(q_all, head, part)))
    wait(arrive[2:6])
    for head in range(HEADS):
        matrix = per_channel(probs[head], spread, same, True)
        put(2 * channels, head, dot(matrix, head_rows(grad_all, head, part)))

    leave = []
    for n, d in enumerate((2, 3, 1, 0)):
        base = (place[0] ^ d) * block
        wait(arrive[6 + 2 * n : 8 + 2 * n])

        def member(i, base=base, d=d):
            hat, spread = channel_hat(x[d, i].astype(f32))
            normed = (hat * gain[...]).astype(bf16)
            qkv = qkv_all[base + i]
            grad_normed = dot(w_qkv_t[...], qkv)
            rows[d, i] = (resid[d, i] + norm_back(grad_normed * gain[...], hat, spread)).astype(bf16)
            g_qkv[...] += dot_t(qkv, normed)
            g_gain[...] += jnp.sum(grad_normed * hat, axis=1, keepdims=True)

        loop(block, member)
        leave += start([pltpu.make_async_copy(rows.at[d], rows_out[d], sout.at[d])])
    late[:channels, :channels] = g_qkv[:channels]
    late[:channels, channels:] = g_qkv[channels : 2 * channels]
    late[channels:, :channels] = g_qkv[2 * channels :]
    late[channels:, channels:] = jnp.broadcast_to(g_gain[...], (channels, channels))
    core = lax.rem(place[0], 2)
    own[...] = late[pl.ds(pl.multiple_of(core * channels, 8), channels), :]
    other[...] = late[pl.ds(pl.multiple_of((1 - core) * channels, 8), channels), :]
    wait(leave)


def call(kernel, operands, outs, scratch, arrive, leave, microseconds):
    def spec(inside):
        return pl.BlockSpec(memory_space=pltpu.VMEM if inside else pltpu.HBM)

    place, *operands = operands
    return pl.pallas_call(
        kernel,
        in_specs=[pl.BlockSpec(memory_space=pltpu.SMEM)] + [spec(t[1]) for t in operands],
        out_specs=[spec(t[1]) for t in outs],
        out_shape=[jax.ShapeDtypeStruct(*t) if near else pltpu.HBM(*t) for t, near in outs],
        scratch_shapes=[pltpu.VMEM(*t) for t in scratch]
        + [pltpu.SemaphoreType.DMA(arrive), pltpu.SemaphoreType.DMA(leave)],
        compiler_params=pltpu.CompilerParams(vmem_limit_bytes=VMEM_LIMIT),
        cost_estimate=pl.CostEstimate(
            flops=0, bytes_accessed=microseconds * 3_600_000, transcendentals=0
        ),
    )(
        place,
        *[
            t if near else pltpu.with_memory_space_constraint(t, pltpu.HBM) for t, near in operands
        ],
    )


def inside(*arrays):
    return [(t, True) for t in arrays]


def outside(*arrays):
    return [(t, False) for t in arrays]


def first_call(place, fields, received, w_qkv, gain, lat):
    block, channels, cells = received[0].shape
    members = block * 4
    field = ((members, channels, cells), bf16)
    sums = ((members, HEADS * members), f32)
    return call(
        first_kernel,
        [place] + outside(fields, *received) + inside(w_qkv, gain, lat),
        outside(field, field, field) + inside(sums),
        [((4, block, channels, cells), bf16), field, field, field],
        (4,),
        (3, 4),
        7,
    )


def far_call(divisor, place, sums, v_all, received, cots, constants):
    members, channels, cells = v_all.shape
    block = members // 4
    inner = constants[2].shape[0]
    field = ((members, channels, cells), bf16)
    one = ((block, channels, cells), bf16)
    pair = ((2, block, channels, cells), bf16)
    wide = (pair[0], f32)
    grads = [((inner, channels), f32)] * 2 + [((channels, channels), f32), ((channels, 1), f32)]
    return call(
        functools.partial(far_kernel, divisor),
        [place] + inside(*sums) + outside(v_all, *received, *cots) + inside(*constants),
        outside(one, one, wide, pair, pair) + inside(*grads),
        [field, field, pair, pair, pair, wide, pair],
        (5,),
        (8,),
        20,
    )


def near_call(place, v_all, fields, x1, cotangent, c1, near, far_grad, constants, grads):
    members, channels, cells = v_all.shape
    block = members // 4
    field = ((members, channels, cells), bf16)
    one = ((block, channels, cells), bf16)
    pair = ((2, block, channels, cells), bf16)
    wide = (pair[0], f32)
    early = grads[0].shape[0] + channels
    packed = ((members + early // 2, 2 * channels), f32)
    return call(
        near_kernel,
        [place]
        + outside(v_all, fields, x1, cotangent, c1, near, far_grad)
        + inside(*constants, *grads),
        outside(one, one, wide, pair) + inside(packed, packed),
        [field, field, pair, pair, pair, pair, wide]
        + [(t.shape, f32) for t in grads]
        + [((early, 2 * channels), f32)],
        (8,),
        (6,),
        20,
    )


def last_call(divisor, place, sums, dots, arrays, constants):
    q_all = arrays[0]
    members, channels, cells = q_all.shape
    block = members // 4
    field = ((members, channels, cells), bf16)
    one = ((block, channels, cells), bf16)
    four = ((4, block, channels, cells), bf16)
    half = ((channels, 2 * channels), f32)
    return call(
        functools.partial(last_kernel, divisor),
        [place] + inside(*sums, *dots) + outside(*arrays) + inside(*constants),
        outside(one, one, one, one) + inside(half, half),
        [field, field, field, four, (four[0], f32), four]
        + [((members, 3 * channels, cells), bf16), ((3 * channels, channels), f32)]
        + [((channels, 1), f32), ((2 * channels, 2 * channels), f32)],
        (14,),
        (4,),
        12,
    )


def exchange(array, distance, axis="member"):
    size = lax.axis_size(axis)
    return lax.ppermute(array, axis, [(i, i ^ distance) for i in range(size)])


def plane_groups():
    size = lax.axis_size("grid")
    return [list(range(part, size, Z_PARTS)) for part in range(Z_PARTS)]


def over_plane(pieces):
    return lax.all_to_all(pieces, "grid", 0, 0, axis_index_groups=plane_groups())


def copies(array):
    return jnp.broadcast_to(array[None], (lax.axis_size("grid") // Z_PARTS,) + array.shape)


def over_z(array):
    array = array + exchange(array, 2)
    return array, exchange(array, 1, "grid")


def together(*arrays):
    return lax.optimization_barrier(arrays)


def shards(fields, cotangent, w_query, w_key, w_value, w_out, w_up, w_down, gain_attn, gain_mlp):
    block, channels, tile = fields.shape
    groups = lax.axis_size("member")
    me = lax.axis_index("member")
    width = tile // groups
    members = block * groups
    inner = w_up.shape[0]
    divisor = sharpness_divisor / ((channels // HEADS) * tile * lax.axis_size("grid"))

    def outgoing(array):
        return [
            lax.dynamic_slice_in_dim(array, (me ^ d) * width, width, axis=2) for d in range(1, groups)
        ]

    def send(pieces, distances):
        return [exchange(piece, d) for piece, d in zip(pieces, distances)]

    def joined(pieces):
        whole_tile = jnp.zeros((block, channels, tile), bf16)
        for d, piece in enumerate(pieces):
            whole_tile = lax.dynamic_update_slice_in_dim(whole_tile, piece, (me ^ d) * width, 2)
        return whole_tile

    position = (me * width).astype(f32) + jnp.arange(width, dtype=f32)
    lat = jnp.cos(lat_span * (position + 0.5) / tile)[None, :]
    w_qkv = jnp.concatenate([w_query, w_key, w_value], axis=0)
    gain_a, gain_m = gain_attn[:, None], gain_mlp[:, None]
    place = me[None].astype(jnp.int32)
    constants = (w_out, w_out.T, w_up, w_up.T, w_down, w_down.T, gain_m)

    far = send(outgoing(fields)[1:], (2, 3))
    x1 = exchange(outgoing(fields)[0], 1)
    cots = outgoing(cotangent)
    far, x1, cots, w_qkv, gain_a, lat = together(far, x1, cots, w_qkv, gain_a, lat)
    received = [x1, *far]
    q_all, k_all, v_all, sums = first_call(place, fields, received, w_qkv, gain_a, lat)
    cots = send(cots, (1, 2, 3))

    sums = jnp.sum(over_plane(copies(sums + exchange(sums, 1))), axis=0)
    sums, cots = together(sums, cots)
    sums = over_z(sums)

    result2, result3, far_resid, far_grad, near, *begun = far_call(
        divisor, place, sums, v_all, received[1:], cots[1:], constants
    )
    result2, result3 = send((result2, result3), (2, 3))
    result0, result1, near_resid, near_grad, own, other = near_call(
        place, v_all, fields, x1, cotangent, cots[0], near, far_grad, constants, begun
    )
    own, other, result2, result3 = together(own, other, result2, result3)
    size = lax.axis_size("grid") // Z_PARTS
    own = own + exchange(other, 1)
    shares = own[members:].reshape(size, -1, own.shape[1])
    pieces = jnp.concatenate([copies(own[:members]), shares], axis=1)
    dots = jnp.sum(over_plane(pieces), axis=0)
    dots = over_z(dots)
    result1 = exchange(result1, 1)

    arrays = (q_all, k_all, near_grad, far_grad, fields, *received, near_resid, far_resid)
    rows0, rows1, rows2, rows3, own, other = last_call(
        divisor, place, sums, dots, arrays, (w_qkv.T, gain_a, lat)
    )
    late, more = over_z(own + exchange(other, 1))
    late = late + more
    late, rows1, rows2, rows3 = together(late, rows1, rows2, rows3)
    rows1, rows2, rows3 = send((rows1, rows2, rows3), (1, 2, 3))
    share = dots[0][members:] + dots[1][members:]
    own_rows = late.shape[0]
    gathered = over_plane(copies(jnp.concatenate([late, share])))
    half = jnp.concatenate(
        [
            jnp.sum(gathered[:, :own_rows], axis=0),
            gathered[:, own_rows:].reshape(-1, late.shape[1]),
        ]
    )
    other = exchange(half, 1)
    core = me % 2
    low = jnp.where(core == 0, half, other)
    high = jnp.where(core == 0, other, half)
    late = jnp.concatenate([low[:own_rows], high[:own_rows]])
    early = jnp.concatenate([low[own_rows:], high[own_rows:]])
    result = joined((result0, result1, result2, result3))
    grad_fields = joined((rows0, rows1, rows2, rows3))
    return (
        result,
        grad_fields,
        late[:channels, :channels],
        late[:channels, channels:],
        late[channels:, :channels],
        early[inner:, :channels],
        early[:inner, :channels],
        early[:inner, channels:].T,
        late[channels:, channels],
        early[inner:, channels],
    )


def solution(mesh):
    split = P("member", None, "grid")
    return jax.shard_map(
        shards,
        mesh=mesh,
        in_specs=(split, split) + (P(),) * 8,
        out_specs=(split, split) + (P(),) * 8,
        check_vma=False,
    )
```

time: 496 us -> 192 us (0.39)
  blocking collectives: 131 us -> 14.3 us
  waiting for transfers between devices: 156 us -> 50.1 us
  matrix products: 90 us -> 0 us
  Pallas kernels: 0 us -> 64.9 us
  local copies, waits for them, and re-layouts: 66.4 us -> 15.5 us
  starting transfers between devices: 21.3 us -> 44 us
  between operations: 14.9 us -> 1.2 us
  other arithmetic: 11.6 us -> 1.22 us
    psum x1 -> x0, waiting for transfers between devices: 138 us -> none  [shards(): summed = lax.psum(pack_sums(joined), ('member', 'grid'))]
    psum x2 -> x0, blocking collectives: 131 us -> none  [the longest x1 68.5 us: shards(): lax.psum(score_terms(query, key), ('member', 'grid')) * attention_divisor]
    dot_general x24 -> x0, matrix products: 90 us -> none  [the longest x6 26.8 us: project_back(): jnp.einsum('oc,mog->mcg', weight_matrix, grad, preferred_element_type=jnp...]
    pallas_call x0 -> x4, Pallas kernels: none -> 64.9 us  [call(): pl.pallas_call(kernel, in_specs=[pl.BlockSpec(memory_space=pltpu.SMEM)] +...]
    ppermute x0 -> x22, waiting for transfers between devices: none -> 39.3 us  [exchange(): return lax.ppermute(array, axis, [(i, i ^ distance) for i in range(size)])]
    unnamed x48 -> x44, local copies, waits for them, and re-layouts: 40.6 us -> 2.51 us
    ppermute x0 -> x22, starting transfers between devices: none -> 35.7 us  [exchange(): return lax.ppermute(array, axis, [(i, i ^ distance) for i in range(size)])]
    all_to_all x0 -> x1, blocking collectives: none -> 14.3 us  [over_plane(): lax.all_to_all(pieces, 'grid', 0, 0, axis_index_groups=plane_groups())]
  transfers between devices with their start and end apart: 5 -> 24, of which waited for: 3 -> 15; matrix products, arithmetic and copies ran while one was open for 15% -> 5% of each run, Pallas kernels for 0% -> 23%
where the time goes in v2:
time: 192 us; the launch traced here: 191 us
  Pallas kernels  64.9 us (34%)
  waiting for transfers between devices  50.1 us (26%)
  starting transfers between devices  44 us (23%)
  local copies, waits for them, and re-layouts  15.5 us (8%)
  blocking collectives  14.3 us (7%)
    pallas_call x4, Pallas kernels, call(): pl.pallas_call(kernel, in_specs=[pl.BlockSpec(memory_space=pltpu.SMEM)] +...  64.9 us
    ppermute x22, waiting for transfers between devices, exchange(): return lax.ppermute(array, axis, [(i, i ^ distance) for i in range(size)])  39.3 us
    ppermute x22, starting transfers between devices, exchange(): return lax.ppermute(array, axis, [(i, i ^ distance) for i in range(size)])  35.7 us
    all_to_all x1, blocking collectives, over_plane(): lax.all_to_all(pieces, 'grid', 0, 0, axis_index_groups=plane_groups())  14.3 us
    all_to_all x2, waiting for transfers between devices, over_plane(): lax.all_to_all(pieces, 'grid', 0, 0, axis_index_groups=plane_groups())  10.8 us
    all_to_all x2, starting transfers between devices, over_plane(): lax.all_to_all(pieces, 'grid', 0, 0, axis_index_groups=plane_groups())  8.29 us
    dynamic_update_slice x8, local copies, waits for them, and re-layouts, joined(): lax.dynamic_update_slice_in_dim(whole_tile, piece, (me ^ d) * width, 2)  5.78 us
    dynamic_slice x2, local copies, waits for them, and re-layouts, outgoing(): lax.dynamic_slice_in_dim(array, (me ^ d) * width, width, axis=2)  3.93 us
  transfers between devices with their start and end apart: 24, of which 15 were waited for; matrix products, arithmetic and copies ran while one was open for 5% of the time, Pallas kernels for 23%

profile of v2, /device:TPU:1, one launch (start us, length us, event | category | flops | bytes accessed | tf_op | source)
XLA Modules:
  0.0 191.3 jit_solution(9286688988366084946)
XLA Ops:
  0.7 2.7 %constant_dynamic-slice_fusion.3 = (bf16[8,64,512]{2,1,0:T(8,128)(2,1)}, bf16[8,64,512]{2,1,0:T(8,128)(2,1)}, bf16[8,64,512]{2,1,0:T(8,128)(2,1)}) fusion(bf16[8,64,2048]{2,1,0:T(8,128)(2,1)} %refs_9_.1, s32[]{:T(128)S(6)} %select_n.43, s32[]{:T(128)S(6)} %select_n.42, s32[]{:T(128)S(6)} %select_n.41), kind=kLoop, calls=%fused_computation.26 | loop fusion | bytes 3145740 | tf_op jit(solution)/shard_map/dynamic_slice | solution.py:532
  3.4 2.5 %collective-permute-start = (bf16[8,64,512]{2,1,0:T(8,128)(2,1)}, bf16[8,64,512]{2,1,0:T(8,128)(2,1)S(1)}, u32[]{:S(2)}, u32[]{:S(2)}) collective-permute-start(bf16[8,64,512]{2,1,0:T(8,128)(2,1)} %get-tuple-element.159), channel_id=1, source_target_pairs={{0,64},{32,96},{64,0},{96,32},{1,65},{33,97},{65,1},{97,33},{2,66}... | collective-permute-start | bytes 1572872 | tf_op jit(solution)/shard_map/ppermute | solution.py:496
  7.3 1.2 constant_dynamic-slice_fusion
  8.6 9.2 %collective-permute-done.x2.refs_4_.refs_11_ = bf16[8,64,512]{2,1,0:T(8,128)(2,1)S(1)} collective-permute-done((bf16[8,64,512]{2,1,0:T(8,128)(2,1)}, bf16[8,64,512]{2,1,0:T(8,128)(2,1)S(1)}, u32[]{:S(2)}, u32[]{:S(2)}) %collective-permute-start) | collective-permute-done | bytes 524320 | tf_op jit(solution)/shard_map/ppermute | solution.py:496
  17.7 11.8 %collective-permute-done.1.x3.refs_5_.refs_12_ = bf16[8,64,512]{2,1,0:T(8,128)(2,1)S(1)} collective-permute-done((bf16[8,64,512]{2,1,0:T(8,128)(2,1)}, bf16[8,64,512]{2,1,0:T(8,128)(2,1)S(1)}, u32[]{:S(2)}, u32[]{:S(2)}) %collective-permute-start.1) | collective-permute-done | bytes 524320 | tf_op jit(solution)/shard_map/ppermute | solution.py:496
  29.6 1.5 collective-permute-start.5
  32.0 7.6 %shard_map.177 = (bf16[32,64,512]{2,1,0:T(8,128)(2,1)}, bf16[32,64,512]{2,1,0:T(8,128)(2,1)}, bf16[32,64,512]{2,1,0:T(8,128)(2,1)}, f32[32,128]{1,0:T(8,128)S(1)}) custom-call(s32[1]{0:T(128)} %bitcast.place.refs_0_, bf16[8,64,2048]{2,1,0:T(8,128)(2,1)} %refs_9_.1, bf16[8,64,512]{2,1,0:T(8,128)(2,1)} %collective-permute-done.2.x1.refs_3_.refs_10_, ...), custom_call_target="tpu_custom_call" | custom-call | bytes 25200000 | tf_op jit(solution)/shard_map/pallas_call | solution.py:386
  40.8 14.3 %all_to_all.15 = f32[16,32,128]{2,1,0:T(8,128)S(1)} all-to-all(f32[16,32,128]{2,1,0:T(8,128)S(1)} %broadcast_in_dim.14), channel_id=1, replica_groups={{0,2,4,6,8,10,12,14,16,18,20,22,24,26,28,30},{1,3,5,7,9,11,13,15,17,19,..., dimensions={0} | all-to-all | bytes 524288 | tf_op jit(solution)/shard_map/all_to_all | solution.py:505
  55.3 1.5 collective-permute-start.7
  56.8 1.1 collective-permute-done.7
  57.9 3.4 %collective-permute-start.8 = (f32[32,128]{1,0:T(8,128)S(1)}, f32[32,128]{1,0:T(8,128)S(1)}, u32[]{:S(2)}, u32[]{:S(2)}) collective-permute-start(f32[32,128]{1,0:T(8,128)S(1)} %add.84.refs_1_), channel_id=1, source_target_pairs={{0,1},{1,0},{2,3},{3,2},{4,5},{5,4},{6,7},{7,6},{8,9},{9,8},{10,11... | collective-permute-start | bytes 49160 | tf_op jit(solution)/shard_map/ppermute | solution.py:496
  62.5 21.8 %shard_map.178 = (bf16[8,64,512]{2,1,0:T(8,128)(2,1)}, bf16[8,64,512]{2,1,0:T(8,128)(2,1)}, f32[2,8,64,512]{3,2,1,0:T(8,128)}, bf16[2,8,64,512]{3,2,1,0:T(8,128)...) custom-call(s32[1]{0:T(128)} %bitcast.place.refs_0_, ...), custom_call_target="tpu_custom_call" | custom-call | bytes 72000000 | tf_op jit(solution)/shard_map/pallas_call | solution.py:386
  85.4 4.3 %collective-permute-start.11 = (bf16[8,64,512]{2,1,0:T(8,128)(2,1)}, bf16[8,64,512]{2,1,0:T(8,128)(2,1)S(1)}, u32[]{:S(2)}, u32[]{:S(2)}) collective-permute-start(bf16[8,64,512]{2,1,0:T(8,128)(2,1)} %get-tuple-element.82), channel_id=1, source_target_pairs={{0,96},{32,64},{64,32},{96,0},{1,97},{33,65},{65,33},{97,1},{2,98}... | collective-permute-start | bytes 1572872 | tf_op jit(solution)/shard_map/ppermute | solution.py:496
  89.7 21.1 %shard_map.179 = (bf16[8,64,512]{2,1,0:T(8,128)(2,1)}, bf16[8,64,512]{2,1,0:T(8,128)(2,1)}, f32[2,8,64,512]{3,2,1,0:T(8,128)}, bf16[2,8,64,512]{3,2,1,0:T(8,128)...) custom-call(s32[1]{0:T(128)} %bitcast.place.refs_0_, bf16[32,64,512]{2,1,0:T(8,128)(2,1)} %get-tuple-element.62.refs_3_.refs_1_, ...), custom_call_target="tpu_custom_call" | custom-call | bytes 72000000 | tf_op jit(solution)/shard_map/pallas_call | solution.py:386
  110.9 1.3 collective-permute-done.12
  113.1 4.7 %all-to-all-start.1 = ((f32[16,42,128]{2,1,0:T(8,128)}), f32[16,42,128]{2,1,0:T(8,128)S(1)}, u32[]{:S(2)}, u32[]{:S(2)}) async-start(f32[16,42,128]{2,1,0:T(8,128)} %pad_maximum_fusion), calls=%async_computation.1 | async-start | bytes 786432 | tf_op jit(solution)/shard_map/all_to_all | solution.py:505
  118.3 8.8 %all-to-all-done.1 = f32[16,42,128]{2,1,0:T(8,128)S(1)} async-done(((f32[16,42,128]{2,1,0:T(8,128)}), f32[16,42,128]{2,1,0:T(8,128)S(1)}, u32[]{:S(2)}, u32[]{:S(2)}) %all-to-all-start.1) | async-done | bytes 344096 | tf_op jit(solution)/shard_map/all_to_all | solution.py:505
  128.2 1.7 collective-permute-done.13
  129.9 3.0 %collective-permute-start.14 = (f32[42,128]{1,0:T(8,128)S(1)}, f32[42,128]{1,0:T(8,128)S(1)}, u32[]{:S(2)}, u32[]{:S(2)}) collective-permute-start(f32[42,128]{1,0:T(8,128)S(1)} %add.87.refs_3_), channel_id=1, source_target_pairs={{0,1},{1,0},{2,3},{3,2},{4,5},{5,4},{6,7},{7,6},{8,9},{9,8},{10,11... | collective-permute-start | bytes 64520 | tf_op jit(solution)/shard_map/ppermute | solution.py:496
  132.9 1.2 collective-permute-done.14.refs_4_
  134.1 14.5 %shard_map.180 = (bf16[8,64,512]{2,1,0:T(8,128)(2,1)}, bf16[8,64,512]{2,1,0:T(8,128)(2,1)}, bf16[8,64,512]{2,1,0:T(8,128)(2,1)}, bf16[8,64,512]{2,1,0:T(8,128)(2...) custom-call(s32[1]{0:T(128)} %bitcast.place.refs_0_, f32[32,128]{1,0:T(8,128)S(1)} %add.84.refs_1_, ...), custom_call_target="tpu_custom_call" | custom-call | bytes 43200000 | tf_op jit(solution)/shard_map/pallas_call | solution.py:386
  148.6 3.8 %collective-permute-start.15 = (f32[64,128]{1,0:T(8,128)S(1)}, f32[64,128]{1,0:T(8,128)S(1)}, u32[]{:S(2)}, u32[]{:S(2)}) collective-permute-start(f32[64,128]{1,0:T(8,128)S(1)} %get-tuple-element.94), channel_id=1, source_target_pairs={{0,32},{32,0},{64,96},{96,64},{1,33},{33,1},{65,97},{97,65},{2,34}... | collective-permute-start | bytes 98312 | tf_op jit(solution)/shard_map/ppermute | solution.py:496
  154.5 1.1 constant_dynamic-update-slice_fusion.7
  156.0 3.0 %collective-permute-start.17 = (f32[64,128]{1,0:T(8,128)S(1)}, f32[64,128]{1,0:T(8,128)S(1)}, u32[]{:S(2)}, u32[]{:S(2)}) collective-permute-start(f32[64,128]{1,0:T(8,128)S(1)} %add.89), channel_id=1, source_target_pairs={{0,1},{1,0},{2,3},{3,2},{4,5},{5,4},{6,7},{7,6},{8,9},{9,8},{10,11... | collective-permute-start | bytes 98312 | tf_op jit(solution)/shard_map/ppermute | solution.py:496
  160.4 2.6 %collective-permute-start.18 = (bf16[8,64,512]{2,1,0:T(8,128)(2,1)}, bf16[8,64,512]{2,1,0:T(8,128)(2,1)}, u32[]{:S(2)}, u32[]{:S(2)}) collective-permute-start(bf16[8,64,512]{2,1,0:T(8,128)(2,1)} %get-tuple-element.98), channel_id=1, source_target_pairs={{0,32},{32,0},{64,96},{96,64},{1,33},{33,1},{65,97},{97,65},{2,34}... | collective-permute-start | bytes 1572872 | tf_op jit(solution)/shard_map/ppermute | solution.py:496
  164.9 3.6 %all-to-all-start.2 = ((f32[16,74,128]{2,1,0:T(8,128)}), f32[16,74,128]{2,1,0:T(8,128)S(1)}, u32[]{:S(2)}, u32[]{:S(2)}) async-start(f32[16,74,128]{2,1,0:T(8,128)} %broadcast_in_dim.33), calls=%async_computation.2 | async-start | bytes 1310720 | tf_op jit(solution)/shard_map/all_to_all | solution.py:505
  168.6 1.2 constant_dynamic-update-slice_fusion.4
  171.4 1.1 constant_dynamic-update-slice_fusion.2
  172.5 4.2 %collective-permute-done.19 = bf16[8,64,512]{2,1,0:T(8,128)(2,1)} collective-permute-done((bf16[8,64,512]{2,1,0:T(8,128)(2,1)}, bf16[8,64,512]{2,1,0:T(8,128)(2,1)}, u32[]{:S(2)}, u32[]{:S(2)}) %collective-permute-start.19) | collective-permute-done | bytes 524320 | tf_op jit(solution)/shard_map/ppermute | solution.py:496
  177.9 2.0 %all-to-all-done.2 = f32[16,74,128]{2,1,0:T(8,128)S(1)} async-done(((f32[16,74,128]{2,1,0:T(8,128)}), f32[16,74,128]{2,1,0:T(8,128)S(1)}, u32[]{:S(2)}, u32[]{:S(2)}) %all-to-all-start.2) | async-done | bytes 606240 | tf_op jit(solution)/shard_map/all_to_all | solution.py:505
  179.9 2.5 %collective-permute-start.21 = (f32[224,128]{1,0:T(8,128)S(1)}, f32[224,128]{1,0:T(8,128)S(1)}, u32[]{:S(2)}, u32[]{:S(2)}) collective-permute-start(f32[224,128]{1,0:T(8,128)S(1)} %pad_maximum_fusion.2), channel_id=1, source_target_pairs={{0,32},{32,0},{64,96},{96,64},{1,33},{33,1},{65,97},{97,65},{2,34}... | collective-permute-start | bytes 344072 | tf_op jit(solution)/shard_map/ppermute | solution.py:496
  182.5 5.6 %collective-permute-done.20 = bf16[8,64,512]{2,1,0:T(8,128)(2,1)S(1)} collective-permute-done((bf16[8,64,512]{2,1,0:T(8,128)(2,1)}, bf16[8,64,512]{2,1,0:T(8,128)(2,1)S(1)}, u32[]{:S(2)}, u32[]{:S(2)}) %collective-permute-start.20) | collective-permute-done | bytes 524320 | tf_op jit(solution)/shard_map/ppermute | solution.py:496
  (110 shorter events, 20.2 us)
Async XLA Ops:
  3.4 28.4 %copy-start.16 = (f32[64]{0:T(128)S(1)}, f32[64]{0:T(128)}, u32[]{:S(2)}) copy-start(f32[64]{0:T(128)} %param.18) | copy-start | bytes 772
  3.4 14.3 %collective-permute-start = (bf16[8,64,512]{2,1,0:T(8,128)(2,1)}, bf16[8,64,512]{2,1,0:T(8,128)(2,1)S(1)}, u32[]{:S(2)}, u32[]{:S(2)}) collective-permute-start(bf16[8,64,512]{2,1,0:T(8,128)(2,1)} %get-tuple-element.159), channel_id=1, source_target_pairs={{0,64},{32,96},{64,0},{96,32},{1,65},{33,97},{65,1},{97,33},{2,66}... | collective-permute-start | bytes 1572872 | tf_op jit(solution)/shard_map/ppermute | solution.py:496
  5.9 23.6 %collective-permute-start.1 = (bf16[8,64,512]{2,1,0:T(8,128)(2,1)}, bf16[8,64,512]{2,1,0:T(8,128)(2,1)S(1)}, u32[]{:S(2)}, u32[]{:S(2)}) collective-permute-start(bf16[8,64,512]{2,1,0:T(8,128)(2,1)} %get-tuple-element.158), channel_id=1, source_target_pairs={{0,96},{32,64},{64,32},{96,0},{1,97},{33,65},{65,33},{97,1},{2,98}... | collective-permute-start | bytes 1572872 | tf_op jit(solution)/shard_map/ppermute | solution.py:496
  6.5 23.0 %collective-permute-start.2 = (bf16[8,64,512]{2,1,0:T(8,128)(2,1)}, bf16[8,64,512]{2,1,0:T(8,128)(2,1)}, u32[]{:S(2)}, u32[]{:S(2)}) collective-permute-start(bf16[8,64,512]{2,1,0:T(8,128)(2,1)} %get-tuple-element.157), channel_id=1, source_target_pairs={{0,32},{32,0},{64,96},{96,64},{1,33},{33,1},{65,97},{97,65},{2,34}... | collective-permute-start | bytes 1572872 | tf_op jit(solution)/shard_map/ppermute | solution.py:496
  17.7 14.2 %copy-start.4 = (bf16[8,64,512]{2,1,0:T(8,128)(2,1)}, bf16[8,64,512]{2,1,0:T(8,128)(2,1)S(1)}, u32[]{:S(2)}) copy-start(bf16[8,64,512]{2,1,0:T(8,128)(2,1)S(1)} %collective-permute-done.x2.refs_4_.refs_11_) | copy-start | bytes 1572868
  29.5 25.7 %collective-permute-start.4 = (bf16[8,64,512]{2,1,0:T(8,128)(2,1)}, bf16[8,64,512]{2,1,0:T(8,128)(2,1)S(1)}, u32[]{:S(2)}, u32[]{:S(2)}) collective-permute-start(bf16[8,64,512]{2,1,0:T(8,128)(2,1)} %get-tuple-element.64), channel_id=1, source_target_pairs={{0,32},{32,0},{64,96},{96,64},{1,33},{33,1},{65,97},{97,65},{2,34}... | collective-permute-start | bytes 1572872 | tf_op jit(solution)/shard_map/ppermute | solution.py:496
  29.6 25.6 %collective-permute-start.5 = (bf16[8,64,512]{2,1,0:T(8,128)(2,1)}, bf16[8,64,512]{2,1,0:T(8,128)(2,1)S(1)}, u32[]{:S(2)}, u32[]{:S(2)}) collective-permute-start(bf16[8,64,512]{2,1,0:T(8,128)(2,1)} %get-tuple-element.65), channel_id=1, source_target_pairs={{0,64},{32,96},{64,0},{96,32},{1,65},{33,97},{65,1},{97,33},{2,66}... | collective-permute-start | bytes 1572872 | tf_op jit(solution)/shard_map/ppermute | solution.py:496
  31.1 24.2 %collective-permute-start.6 = (bf16[8,64,512]{2,1,0:T(8,128)(2,1)}, bf16[8,64,512]{2,1,0:T(8,128)(2,1)S(1)}, u32[]{:S(2)}, u32[]{:S(2)}) collective-permute-start(bf16[8,64,512]{2,1,0:T(8,128)(2,1)} %get-tuple-element.66), channel_id=1, source_target_pairs={{0,96},{32,64},{64,32},{96,0},{1,97},{33,65},{65,33},{97,1},{2,98}... | collective-permute-start | bytes 1572872 | tf_op jit(solution)/shard_map/ppermute | solution.py:496
  31.9 29.4 %copy-start.1 = (bf16[64,256]{1,0:T(8,128)(2,1)S(1)}, bf16[64,256]{1,0:T(8,128)(2,1)}, u32[]{:S(2)}) copy-start(bf16[64,256]{1,0:T(8,128)(2,1)} %refs_12_.3) | copy-start | bytes 98308
  31.9 29.6 %copy-start = (bf16[256,64]{0,1:T(8,128)(2,1)S(1)}, bf16[256,64]{0,1:T(8,128)(2,1)}, u32[]{:S(2)}) copy-start(bf16[256,64]{0,1:T(8,128)(2,1)} %param.16) | copy-start | bytes 98308
  31.9 29.7 %copy-start.17 = (f32[64]{0:T(128)S(1)}, f32[64]{0:T(128)}, u32[]{:S(2)}) copy-start(f32[64]{0:T(128)} %param.19) | copy-start | bytes 772
  31.9 29.8 %copy-start.2 = (bf16[64,64]{1,0:T(8,128)(2,1)S(1)}, bf16[64,64]{1,0:T(8,128)(2,1)}, u32[]{:S(2)}) copy-start(bf16[64,64]{1,0:T(8,128)(2,1)} %refs_8_.3) | copy-start | bytes 24580
  39.5 1.3 collective-permute-start.3
  55.2 29.1 %copy-start.8 = (bf16[8,64,512]{2,1,0:T(8,128)(2,1)}, bf16[8,64,512]{2,1,0:T(8,128)(2,1)S(1)}, u32[]{:S(2)}) copy-start(bf16[8,64,512]{2,1,0:T(8,128)(2,1)S(1)} %collective-permute-done.4.refs_5_) | copy-start | bytes 1572868
  55.2 7.3 %copy-start.9 = (bf16[8,64,512]{2,1,0:T(8,128)(2,1)}, bf16[8,64,512]{2,1,0:T(8,128)(2,1)S(1)}, u32[]{:S(2)}) copy-start(bf16[8,64,512]{2,1,0:T(8,128)(2,1)S(1)} %collective-permute-done.5.refs_6_) | copy-start | bytes 1572868
  55.3 2.7 %collective-permute-start.7 = (f32[32,128]{1,0:T(8,128)S(1)}, f32[32,128]{1,0:T(8,128)S(1)}, u32[]{:S(2)}, u32[]{:S(2)}) collective-permute-start(f32[32,128]{1,0:T(8,128)S(1)} %reduce_sum.27), channel_id=1, source_target_pairs={{0,64},{32,96},{64,0},{96,32},{1,65},{33,97},{65,1},{97,33},{2,66}... | collective-permute-start | bytes 49160 | tf_op jit(solution)/shard_map/ppermute | solution.py:496
  57.9 4.5 %collective-permute-start.8 = (f32[32,128]{1,0:T(8,128)S(1)}, f32[32,128]{1,0:T(8,128)S(1)}, u32[]{:S(2)}, u32[]{:S(2)}) collective-permute-start(f32[32,128]{1,0:T(8,128)S(1)} %add.84.refs_1_), channel_id=1, source_target_pairs={{0,1},{1,0},{2,3},{3,2},{4,5},{5,4},{6,7},{7,6},{8,9},{9,8},{10,11... | collective-permute-start | bytes 49160 | tf_op jit(solution)/shard_map/ppermute | solution.py:496
  84.3 26.5 %collective-permute-start.10 = (bf16[8,64,512]{2,1,0:T(8,128)(2,1)}, bf16[8,64,512]{2,1,0:T(8,128)(2,1)S(1)}, u32[]{:S(2)}, u32[]{:S(2)}) collective-permute-start(bf16[8,64,512]{2,1,0:T(8,128)(2,1)} %get-tuple-element.81), channel_id=1, source_target_pairs={{0,64},{32,96},{64,0},{96,32},{1,65},{33,97},{65,1},{97,33},{2,66}... | collective-permute-start | bytes 1572872 | tf_op jit(solution)/shard_map/ppermute | solution.py:496
  85.4 25.4 %collective-permute-start.11 = (bf16[8,64,512]{2,1,0:T(8,128)(2,1)}, bf16[8,64,512]{2,1,0:T(8,128)(2,1)S(1)}, u32[]{:S(2)}, u32[]{:S(2)}) collective-permute-start(bf16[8,64,512]{2,1,0:T(8,128)(2,1)} %get-tuple-element.82), channel_id=1, source_target_pairs={{0,96},{32,64},{64,32},{96,0},{1,97},{33,65},{65,33},{97,1},{2,98}... | collective-permute-start | bytes 1572872 | tf_op jit(solution)/shard_map/ppermute | solution.py:496
  110.8 1.4 collective-permute-start.12
  113.1 14.0 %all-to-all-start.1 = ((f32[16,42,128]{2,1,0:T(8,128)}), f32[16,42,128]{2,1,0:T(8,128)S(1)}, u32[]{:S(2)}, u32[]{:S(2)}) async-start(f32[16,42,128]{2,1,0:T(8,128)} %pad_maximum_fusion), calls=%async_computation.1 | async-start | bytes 786432 | tf_op jit(solution)/shard_map/all_to_all | solution.py:505
  117.8 41.3 %collective-permute-start.9 = (bf16[8,64,512]{2,1,0:T(8,128)(2,1)}, bf16[8,64,512]{2,1,0:T(8,128)(2,1)}, u32[]{:S(2)}, u32[]{:S(2)}) collective-permute-start(bf16[8,64,512]{2,1,0:T(8,128)(2,1)} %get-tuple-element.78), channel_id=1, source_target_pairs={{0,32},{32,0},{64,96},{96,64},{1,33},{33,1},{65,97},{97,65},{2,34}... | collective-permute-start | bytes 1572872 | tf_op jit(solution)/shard_map/ppermute | solution.py:496
  127.1 2.8 %collective-permute-start.13 = (f32[42,128]{1,0:T(8,128)S(1)}, f32[42,128]{1,0:T(8,128)S(1)}, u32[]{:S(2)}, u32[]{:S(2)}) collective-permute-start(f32[42,128]{1,0:T(8,128)S(1)} %reduce_sum.28), channel_id=1, source_target_pairs={{0,64},{32,96},{64,0},{96,32},{1,65},{33,97},{65,1},{97,33},{2,66}... | collective-permute-start | bytes 64520 | tf_op jit(solution)/shard_map/ppermute | solution.py:496
  129.9 4.2 %collective-permute-start.14 = (f32[42,128]{1,0:T(8,128)S(1)}, f32[42,128]{1,0:T(8,128)S(1)}, u32[]{:S(2)}, u32[]{:S(2)}) collective-permute-start(f32[42,128]{1,0:T(8,128)S(1)} %add.87.refs_3_), channel_id=1, source_target_pairs={{0,1},{1,0},{2,3},{3,2},{4,5},{5,4},{6,7},{7,6},{8,9},{9,8},{10,11... | collective-permute-start | bytes 64520 | tf_op jit(solution)/shard_map/ppermute | solution.py:496
  148.6 4.7 %collective-permute-start.15 = (f32[64,128]{1,0:T(8,128)S(1)}, f32[64,128]{1,0:T(8,128)S(1)}, u32[]{:S(2)}, u32[]{:S(2)}) collective-permute-start(f32[64,128]{1,0:T(8,128)S(1)} %get-tuple-element.94), channel_id=1, source_target_pairs={{0,32},{32,0},{64,96},{96,64},{1,33},{33,1},{65,97},{97,65},{2,34}... | collective-permute-start | bytes 98312 | tf_op jit(solution)/shard_map/ppermute | solution.py:496
  153.3 2.8 %collective-permute-start.16 = (f32[64,128]{1,0:T(8,128)S(1)}, f32[64,128]{1,0:T(8,128)S(1)}, u32[]{:S(2)}, u32[]{:S(2)}) collective-permute-start(f32[64,128]{1,0:T(8,128)S(1)} %add.88), channel_id=1, source_target_pairs={{0,64},{32,96},{64,0},{96,32},{1,65},{33,97},{65,1},{97,33},{2,66}... | collective-permute-start | bytes 98312 | tf_op jit(solution)/shard_map/ppermute | solution.py:496
  156.0 4.3 %collective-permute-start.17 = (f32[64,128]{1,0:T(8,128)S(1)}, f32[64,128]{1,0:T(8,128)S(1)}, u32[]{:S(2)}, u32[]{:S(2)}) collective-permute-start(f32[64,128]{1,0:T(8,128)S(1)} %add.89), channel_id=1, source_target_pairs={{0,1},{1,0},{2,3},{3,2},{4,5},{5,4},{6,7},{7,6},{8,9},{9,8},{10,11... | collective-permute-start | bytes 98312 | tf_op jit(solution)/shard_map/ppermute | solution.py:496
  160.4 11.0 %collective-permute-start.18 = (bf16[8,64,512]{2,1,0:T(8,128)(2,1)}, bf16[8,64,512]{2,1,0:T(8,128)(2,1)}, u32[]{:S(2)}, u32[]{:S(2)}) collective-permute-start(bf16[8,64,512]{2,1,0:T(8,128)(2,1)} %get-tuple-element.98), channel_id=1, source_target_pairs={{0,32},{32,0},{64,96},{96,64},{1,33},{33,1},{65,97},{97,65},{2,34}... | collective-permute-start | bytes 1572872 | tf_op jit(solution)/shard_map/ppermute | solution.py:496
  163.0 13.8 %collective-permute-start.19 = (bf16[8,64,512]{2,1,0:T(8,128)(2,1)}, bf16[8,64,512]{2,1,0:T(8,128)(2,1)}, u32[]{:S(2)}, u32[]{:S(2)}) collective-permute-start(bf16[8,64,512]{2,1,0:T(8,128)(2,1)} %get-tuple-element.99), channel_id=1, source_target_pairs={{0,64},{32,96},{64,0},{96,32},{1,65},{33,97},{65,1},{97,33},{2,66}... | collective-permute-start | bytes 1572872 | tf_op jit(solution)/shard_map/ppermute | solution.py:496
  164.9 15.0 %all-to-all-start.2 = ((f32[16,74,128]{2,1,0:T(8,128)}), f32[16,74,128]{2,1,0:T(8,128)S(1)}, u32[]{:S(2)}, u32[]{:S(2)}) async-start(f32[16,74,128]{2,1,0:T(8,128)} %broadcast_in_dim.33), calls=%async_computation.2 | async-start | bytes 1310720 | tf_op jit(solution)/shard_map/all_to_all | solution.py:505
  169.7 18.3 %collective-permute-start.20 = (bf16[8,64,512]{2,1,0:T(8,128)(2,1)}, bf16[8,64,512]{2,1,0:T(8,128)(2,1)S(1)}, u32[]{:S(2)}, u32[]{:S(2)}) collective-permute-start(bf16[8,64,512]{2,1,0:T(8,128)(2,1)} %get-tuple-element.100), channel_id=1, source_target_pairs={{0,96},{32,64},{64,32},{96,0},{1,97},{33,65},{65,33},{97,1},{2,98}... | collective-permute-start | bytes 1572872 | tf_op jit(solution)/shard_map/ppermute | solution.py:496
  179.9 8.2 %collective-permute-start.21 = (f32[224,128]{1,0:T(8,128)S(1)}, f32[224,128]{1,0:T(8,128)S(1)}, u32[]{:S(2)}, u32[]{:S(2)}) collective-permute-start(f32[224,128]{1,0:T(8,128)S(1)} %pad_maximum_fusion.2), channel_id=1, source_target_pairs={{0,32},{32,0},{64,96},{96,64},{1,33},{33,1},{65,97},{97,65},{2,34}... | collective-permute-start | bytes 344072 | tf_op jit(solution)/shard_map/ppermute | solution.py:496
  (10 other events, 44.8 us)
